TPU v7x, 32 devices: a whole 2x2x4 slice. The times are simulated.
32 devices in a mesh: dp: 4 (over y, x), row: 4 (over z), col: 2 (over core).
Axes of the slice: x: 2, y: 2, z: 4, core: 2. Of those that a mesh axis runs over, the one named last changes fastest.
Arguments:
- inputs: bfloat16 [8192, 1024], P(('dp', 'col'), 'row'), may hold values from -6 to 6
- segments: int32 [4, 2048], P('dp'), may hold values from 0 to 7, never falling along the last dimension, each value on 1 to 1537 neighbouring positions
- ln_gain: bfloat16 [1024], P('row'), may hold values from 0.099609375 to 1.8984375
- ln_bias: bfloat16 [1024], P('row'), may hold values from -1.75 to 1.75
- w_qkv: bfloat16 [1024, 3, 1024], P('row', None, 'col'), may hold values from -0.1875 to 0.1875
- b_qkv: bfloat16 [3, 1024], P(None, 'col'), may hold values from -0.3125 to 0.3125
- w_out: bfloat16 [1024, 1024], P('col', 'row'), may hold values from -0.75 to 0.75
- w_up: bfloat16 [1024, 4096], P('row', 'col'), may hold values from -0.1875 to 0.1875
- b_up: bfloat16 [4096], P('col'), may hold values from -1.75 to 1.75
- w_down: bfloat16 [4096, 1024], P('col', 'row'), may hold values from -0.09375 to 0.09375
- out_bias: bfloat16 [1024], P('row'), may hold values from -1.75 to 1.75
- cotangent: bfloat16 [8192, 1024], P(('dp', 'col'), 'row'), may hold values from -8 to 8
Outputs:
- layer_out: bfloat16 [8192, 1024], P(('dp', 'col'), 'row')
- grad_inputs: float32 [8192, 1024], P(('dp', 'col'), 'row')
- grad_ln_gain: float32 [1024], P('row')
- grad_ln_bias: float32 [1024], P('row')
- grad_w_qkv: float32 [1024, 3, 1024], P('row', None, 'col')
- grad_b_qkv: float32 [3, 1024], P(None, 'col')
- grad_w_out: float32 [1024, 1024], P('col', 'row')
- grad_w_up: float32 [1024, 4096], P('row', 'col')
- grad_b_up: float32 [4096], P('col')
- grad_w_down: float32 [4096, 1024], P('col', 'row')
- grad_out_bias: float32 [1024], P('row')
Inputs may be any that keep to these rules, and one draw needn't show every extreme that they name: `segments`: in each sequence the document numbers start at 0 and never fall; every document holds 1 to 1537 tokens and one holds exactly 1537.
All inputs are finite; a program needn't handle non-finite values.
Results may differ from a plain program's by a relative error of at most 0.03.
Values may be sent and summed in bfloat16 or wider, within the bound.
A program may use at most 128 MiB of HBM per device.

v0:
```python
import math

import jax
import jax.numpy as jnp
from jax import lax
from jax.sharding import PartitionSpec as P

D = 1024
HD = 64
ROT = 16
SEQ_LEN = 2048


EPSILON = 1e-05
MASKED = -1000000000.0
FLOOR_INIT = -1e30


def doc_positions(labels):
    token_index = jnp.arange(labels.shape[1], dtype=jnp.int32)
    flags = jnp.concatenate(
        [jnp.ones((labels.shape[0], 1), dtype=jnp.bool_), labels[:, 1:] != labels[:, :-1]], 1
    )
    starts = lax.cummax(jnp.where(flags, token_index[None, :], 0), axis=1)
    return token_index[None, :] - starts


def rotate(tensor_in, positions):
    half_rot = ROT // 2
    inverse = 10000.0 ** (-(jnp.arange(half_rot, dtype=jnp.float32) * 2.0 / ROT))
    angles = positions.astype(jnp.float32)[:, None] * inverse[None, :]
    cosines = jnp.cos(angles)[:, None, :]
    sine_vals = jnp.sin(angles)[:, None, :]
    first_half = tensor_in[..., :half_rot]
    second_half = tensor_in[..., half_rot:ROT]
    rest_dims = tensor_in[..., ROT:]
    return jnp.concatenate(
        [
            first_half * cosines - second_half * sine_vals,
            second_half * cosines + first_half * sine_vals,
            rest_dims,
        ],
        -1,
    )


def slice_rows(array_in, first_row, row_count, axis_num=0):
    return lax.dynamic_slice_in_dim(array_in, first_row, row_count, axis_num)


def put_rows(array_in, update, first_row, axis_num=0):
    return lax.dynamic_update_slice_in_dim(array_in, update, first_row, axis_num)


def block_pairs(query_blocks, key_blocks):
    q_list = jnp.repeat(jnp.arange(query_blocks, dtype=jnp.int32), key_blocks)
    k_list = jnp.tile(jnp.arange(key_blocks, dtype=jnp.int32), query_blocks)
    return (q_list, k_list)


def per_device(
    inputs, segments, ln_gain, ln_bias, w_qkv, b_qkv, w_out, w_up, b_up, w_down, out_bias, cotangent
):
    local_rows, feature_cols = inputs.shape
    part_count = lax.axis_size("row")
    row_index = lax.axis_index("row")
    head_cols = w_qkv.shape[2]
    head_count = head_cols // HD
    group_seqs = segments.shape[0]
    all_rows = group_seqs * SEQ_LEN
    span = all_rows // part_count
    query_blocks = span // span
    score_scale = 1.0 / math.sqrt(HD)
    labels = (segments + (jnp.arange(group_seqs, dtype=jnp.int32) * SEQ_LEN)[:, None]).reshape(-1)
    positions = doc_positions(segments).reshape(-1)
    token_index = jnp.arange(all_rows, dtype=jnp.int32)
    my_labels = slice_rows(labels, row_index * span, span)
    my_index = slice_rows(token_index, row_index * span, span)
    my_positions = slice_rows(positions, row_index * span, span)
    float_in = inputs.astype(jnp.float32)
    ln_sums = lax.psum((jnp.sum(float_in, 1), jnp.sum(float_in * float_in, 1)), "row")
    row_mean = ln_sums[0] / D
    row_var = ln_sums[1] / D - row_mean * row_mean
    inv_std = lax.rsqrt(row_var + EPSILON)
    centred = (float_in - row_mean[:, None]) * inv_std[:, None]
    normed = (centred * ln_gain.astype(jnp.float32) + ln_bias.astype(jnp.float32)).astype(
        jnp.bfloat16
    )
    gathered_hidden = lax.all_gather(normed, "col", axis=0, tiled=True)
    first_weights = jnp.concatenate([w_qkv.reshape(feature_cols, 3 * head_cols), w_up], 1)
    first_bias = jnp.concatenate(
        [b_qkv.reshape(3 * head_cols).astype(jnp.float32), b_up.astype(jnp.float32)]
    )
    first_out = (
        lax.psum_scatter(
            jnp.dot(
                slice_rows(gathered_hidden, jnp.int32(0), lax.axis_size("row") * span),
                first_weights,
                preferred_element_type=jnp.float32,
            ).astype(jnp.bfloat16),
            "row",
            scatter_dimension=0,
            tiled=True,
        ).astype(jnp.float32)
        + first_bias
    )

    def rotate_mine(tensor_in):
        return rotate(tensor_in, my_positions)

    query_lin = first_out[:, :head_cols].reshape(span, head_count, HD)
    key_lin = first_out[:, head_cols : 2 * head_cols].reshape(span, head_count, HD)
    query = rotate_mine(query_lin).astype(jnp.bfloat16)
    key_rows = rotate_mine(key_lin).astype(jnp.bfloat16)
    value_rows = (
        first_out[:, 2 * head_cols : 3 * head_cols]
        .reshape(span, head_count, HD)
        .astype(jnp.bfloat16)
    )
    up_lin = first_out[:, 3 * head_cols :]
    activated = jax.nn.gelu(up_lin, approximate=False).astype(jnp.bfloat16)

    def over_keys(fold_step, initial):
        return fold_step(
            initial,
            (
                lax.all_gather(key_rows, "row", axis=0, tiled=True),
                lax.all_gather(value_rows, "row", axis=0, tiled=True),
            ),
            jnp.int32(0),
        )

    def key_setup(pieces, first_row):
        row_count = pieces[0].shape[0]
        piece_labels = slice_rows(labels, first_row, row_count)
        piece_index = slice_rows(token_index, first_row, row_count)
        return (row_count, span, piece_labels, piece_index)

    def block_live(piece_labels, piece_index, key_size, q_block, k_block):
        q_labels = slice_rows(my_labels, q_block * span, span)
        q_index = slice_rows(my_index, q_block * span, span)
        k_labels = slice_rows(piece_labels, k_block * key_size, key_size)
        k_index = slice_rows(piece_index, k_block * key_size, key_size)
        return (
            (jnp.max(q_index) >= jnp.min(k_index))
            & (jnp.min(q_labels) <= jnp.max(k_labels))
            & (jnp.min(k_labels) <= jnp.max(q_labels))
        )

    def block_scores(pieces, piece_labels, piece_index, key_size, q_block, k_block):
        q_start = q_block * span
        k_start = k_block * key_size
        q_labels = slice_rows(my_labels, q_start, span)
        q_index = slice_rows(my_index, q_start, span)
        k_labels = slice_rows(piece_labels, k_start, key_size)
        k_index = slice_rows(piece_index, k_start, key_size)
        q_block_rows = slice_rows(query, q_start, span)
        k_block_rows = slice_rows(pieces[0], k_start, key_size)
        v_block_rows = slice_rows(pieces[1], k_start, key_size)
        scores = (
            jnp.einsum(
                "qhd,khd->hqk", q_block_rows, k_block_rows, preferred_element_type=jnp.float32
            )
            * score_scale
        )
        allowed = (q_labels[:, None] == k_labels[None, :]) & (k_index[None, :] <= q_index[:, None])
        scores = jnp.where(allowed[None], scores, MASKED)
        return (q_start, k_start, scores, q_block_rows, k_block_rows, v_block_rows)

    def forward_piece(running, pieces, first_row):
        row_count, key_size, piece_labels, piece_index = key_setup(pieces, first_row)
        q_list, k_list = block_pairs(query_blocks, row_count // key_size)

        def forward_pair_step(current, pair_ids):
            q_block, k_block = pair_ids

            def update(inner_state):
                row_max, row_sum, row_acc = inner_state
                q_start, k_start, scores, q_block_rows, k_block_rows, v_block_rows = block_scores(
                    pieces, piece_labels, piece_index, key_size, q_block, k_block
                )
                old_max = slice_rows(row_max, q_start, span, 1)
                new_max = jnp.maximum(old_max, jnp.max(scores, -1))
                weights = jnp.exp(scores - new_max[..., None])
                keep_part = jnp.exp(old_max - new_max)
                new_sum = slice_rows(row_sum, q_start, span, 1) * keep_part + jnp.sum(weights, -1)
                added = jnp.einsum(
                    "hqk,khd->hqd",
                    weights.astype(jnp.bfloat16),
                    v_block_rows,
                    preferred_element_type=jnp.float32,
                )
                new_acc = slice_rows(row_acc, q_start, span, 1) * keep_part[..., None] + added
                return (
                    put_rows(row_max, new_max, q_start, 1),
                    put_rows(row_sum, new_sum, q_start, 1),
                    put_rows(row_acc, new_acc, q_start, 1),
                )

            def forward_unchanged(inner_state):
                return inner_state

            is_live = block_live(piece_labels, piece_index, key_size, q_block, k_block)
            return (lax.cond(is_live, update, forward_unchanged, current), None)

        result, _ = lax.scan(forward_pair_step, running, (q_list, k_list))
        return result

    forward_init = (
        jnp.full((head_count, span), FLOOR_INIT, jnp.float32),
        jnp.zeros((head_count, span), jnp.float32),
        jnp.zeros((head_count, span, HD), jnp.float32),
    )
    row_max, row_sum, row_acc = over_keys(forward_piece, forward_init)
    log_total = row_max + jnp.log(row_sum)
    attention_raw = jnp.transpose(row_acc / row_sum[..., None], (1, 0, 2)).reshape(span, head_cols)
    attended = attention_raw.astype(jnp.bfloat16)
    joined = jnp.concatenate(
        (
            lax.all_gather(attended, "row", axis=0, tiled=True),
            lax.all_gather(activated, "row", axis=0, tiled=True),
        ),
        1,
    )
    second_weights = jnp.concatenate([w_out, w_down], 0)
    partial_out = lax.psum_scatter(
        jnp.dot(
            slice_rows(joined, jnp.int32(0), lax.axis_size("col") * local_rows),
            second_weights,
            preferred_element_type=jnp.float32,
        ).astype(jnp.bfloat16),
        "col",
        scatter_dimension=0,
        tiled=True,
    ).astype(jnp.float32)
    layer_out = (float_in + partial_out + out_bias.astype(jnp.float32)).astype(jnp.bfloat16)
    grad_full = lax.all_gather(cotangent, "col", axis=0, tiled=True)
    grad_out_bias = jnp.sum(grad_full, 0, dtype=jnp.float32)
    grad_second = lax.dot_general(
        joined, grad_full, (((0,), (0,)), ((), ())), preferred_element_type=jnp.float32
    )
    branch_back = lax.psum_scatter(
        lax.dot_general(
            slice_rows(grad_full, jnp.int32(0), lax.axis_size("row") * span),
            second_weights,
            (((1,), (1,)), ((), ())),
            preferred_element_type=jnp.float32,
        ).astype(jnp.bfloat16),
        "row",
        scatter_dimension=0,
        tiled=True,
    ).astype(jnp.float32)
    d_attended = branch_back[:, :head_cols].astype(jnp.bfloat16)
    d_activated = branch_back[:, head_cols:]
    _, gelu_back = jax.vjp(lambda tensor_in: jax.nn.gelu(tensor_in, approximate=False), up_lin)
    d_up = gelu_back(d_activated)[0].astype(jnp.bfloat16)
    d_out_heads = d_attended.reshape(span, head_count, HD)
    row_delta = jnp.transpose(
        jnp.sum((d_attended.astype(jnp.float32) * attention_raw).reshape(span, head_count, HD), -1)
    )

    def backward_piece(running, pieces, first_row):
        d_query_acc, d_key_all, d_value_all = running
        row_count, key_size, piece_labels, piece_index = key_setup(pieces, first_row)
        q_list, k_list = block_pairs(query_blocks, row_count // key_size)
        zero_keys = jnp.zeros((row_count, head_count, HD), jnp.float32)

        def backward_pair_step(current, pair_ids):
            q_block, k_block = pair_ids

            def update(inner_state):
                d_query_run, d_key_run, d_value_run = inner_state
                q_start, k_start, scores, q_block_rows, k_block_rows, v_block_rows = block_scores(
                    pieces, piece_labels, piece_index, key_size, q_block, k_block
                )
                probs_full = jnp.exp(scores - slice_rows(log_total, q_start, span, 1)[..., None])
                d_out_block = slice_rows(d_out_heads, q_start, span)
                d_probs = jnp.einsum(
                    "qhd,khd->hqk", d_out_block, v_block_rows, preferred_element_type=jnp.float32
                )
                d_scores = (
                    probs_full * (d_probs - slice_rows(row_delta, q_start, span, 1)[..., None])
                ).astype(jnp.bfloat16)
                q_added = (
                    jnp.einsum(
                        "hqk,khd->qhd", d_scores, k_block_rows, preferred_element_type=jnp.float32
                    )
                    * score_scale
                )
                k_added = (
                    jnp.einsum(
                        "hqk,qhd->khd", d_scores, q_block_rows, preferred_element_type=jnp.float32
                    )
                    * score_scale
                )
                v_added = jnp.einsum(
                    "hqk,qhd->khd",
                    probs_full.astype(jnp.bfloat16),
                    d_out_block,
                    preferred_element_type=jnp.float32,
                )
                return (
                    put_rows(
                        d_query_run, slice_rows(d_query_run, q_start, span) + q_added, q_start
                    ),
                    put_rows(
                        d_key_run, slice_rows(d_key_run, k_start, key_size) + k_added, k_start
                    ),
                    put_rows(
                        d_value_run, slice_rows(d_value_run, k_start, key_size) + v_added, k_start
                    ),
                )

            def backward_unchanged(inner_state):
                return inner_state

            is_live = block_live(piece_labels, piece_index, key_size, q_block, k_block)
            return (lax.cond(is_live, update, backward_unchanged, current), None)

        scanned, _ = lax.scan(
            backward_pair_step, (d_query_acc, zero_keys, zero_keys), (q_list, k_list)
        )
        d_query_acc, key_part, value_part = scanned
        d_key_all = put_rows(d_key_all, key_part, first_row)
        d_value_all = put_rows(d_value_all, value_part, first_row)
        return (d_query_acc, d_key_all, d_value_all)

    backward_init = (
        jnp.zeros((span, head_count, HD), jnp.float32),
        jnp.zeros((all_rows, head_count, HD), jnp.float32),
        jnp.zeros((all_rows, head_count, HD), jnp.float32),
    )
    d_query_rot, d_key_total, d_value_total = over_keys(backward_piece, backward_init)
    d_key_rot, d_value_mine = (
        lax.psum_scatter(
            d_key_total.reshape(all_rows, head_cols).astype(jnp.bfloat16),
            "row",
            scatter_dimension=0,
            tiled=True,
        ).astype(jnp.float32),
        lax.psum_scatter(
            d_value_total.reshape(all_rows, head_cols).astype(jnp.bfloat16),
            "row",
            scatter_dimension=0,
            tiled=True,
        ).astype(jnp.float32),
    )
    _, query_back = jax.vjp(rotate_mine, query_lin)
    _, key_back = jax.vjp(rotate_mine, key_lin)
    d_query_lin = query_back(d_query_rot)[0].reshape(span, head_cols).astype(jnp.bfloat16)
    d_key_lin = (
        key_back(d_key_rot.reshape(span, head_count, HD))[0]
        .reshape(span, head_cols)
        .astype(jnp.bfloat16)
    )
    d_first = jnp.concatenate([d_query_lin, d_key_lin, d_value_mine.astype(jnp.bfloat16), d_up], 1)
    d_first_full = lax.all_gather(d_first, "row", axis=0, tiled=True)
    grad_first_bias = jnp.sum(d_first_full, 0, dtype=jnp.float32)
    grad_first = lax.dot_general(
        gathered_hidden, d_first_full, (((0,), (0,)), ((), ())), preferred_element_type=jnp.float32
    )
    d_normed = lax.psum_scatter(
        lax.dot_general(
            slice_rows(d_first_full, jnp.int32(0), lax.axis_size("col") * local_rows),
            first_weights,
            (((1,), (1,)), ((), ())),
            preferred_element_type=jnp.float32,
        ).astype(jnp.bfloat16),
        "col",
        scatter_dimension=0,
        tiled=True,
    ).astype(jnp.float32)
    d_centred = d_normed * ln_gain.astype(jnp.float32)
    grad_stats = lax.psum((jnp.sum(d_centred, 1), jnp.sum(d_centred * centred, 1)), "row")
    grad_inputs = inv_std[:, None] * (
        d_centred - grad_stats[0][:, None] / D - centred * grad_stats[1][:, None] / D
    ) + cotangent.astype(jnp.float32)
    summed = (
        lax.psum(grad_first.astype(jnp.bfloat16), "dp").astype(jnp.float32),
        lax.psum(grad_second.astype(jnp.bfloat16), "dp").astype(jnp.float32),
        lax.psum(grad_first_bias.astype(jnp.bfloat16), "dp").astype(jnp.float32),
        lax.psum(grad_out_bias.astype(jnp.bfloat16), "dp").astype(jnp.float32),
    )
    norm_grads = lax.psum((jnp.sum(d_normed * centred, 0), jnp.sum(d_normed, 0)), ("dp", "col"))
    grad_w_qkv = summed[0][:, : 3 * head_cols].reshape(feature_cols, 3, head_cols)
    grad_w_up = summed[0][:, 3 * head_cols :]
    grad_w_out = summed[1][:head_cols]
    grad_w_down = summed[1][head_cols:]
    grad_b_qkv = summed[2][: 3 * head_cols].reshape(3, head_cols)
    grad_b_up = summed[2][3 * head_cols :]
    return (
        layer_out,
        grad_inputs,
        norm_grads[0],
        norm_grads[1],
        grad_w_qkv,
        grad_b_qkv,
        grad_w_out,
        grad_w_up,
        grad_b_up,
        grad_w_down,
        summed[3],
    )


def solution(mesh):
    placed = (
        P(("dp", "col"), "row"),
        P("dp", None),
        P("row"),
        P("row"),
        P("row", None, "col"),
        P(None, "col"),
        P("col", "row"),
        P("row", "col"),
        P("col"),
        P("col", "row"),
        P("row"),
        P(("dp", "col"), "row"),
    )
    return jax.shard_map(
        per_device,
        mesh=mesh,
        in_specs=placed,
        out_specs=(
            P(("dp", "col"), "row"),
            P(("dp", "col"), "row"),
            P("row"),
            P("row"),
            P("row", None, "col"),
            P(None, "col"),
            P("col", "row"),
            P("row", "col"),
            P("col"),
            P("col", "row"),
            P("row"),
        ),
        check_vma=False,
    )
```

profile of v0, /device:TPU:0, one launch (start us, length us, event | category | flops | bytes accessed | tf_op | source)
XLA Modules:
  0.0 1416.0 jit_solution(3553732519161268901)
XLA Ops:
  10.0 13.7 all-reduce.8
  28.5 4.9 all-gather.8.cloned.1.call-done
  33.4 8.6 convolution_convert_fusion
  45.2 6.7 fusion.46
  52.6 241.8 %reduce-scatter.7.cloned.1.call-done = bf16[512,3584]{1,0:T(8,128)(2,1)} async-done(((bf16[2048,3584]{1,0:T(8,128)(2,1)}), bf16[512,3584]{1,0:T(8,128)(2,1)}) %reduce-scatter.7.cloned.1.call-update) | async-done | bytes 3670032 | tf_op jit(solution)/shard_map/reduce_scatter | solution.py:95
  310.2 165.5 %reduce-scatter.11.cloned.1.call-done = bf16[512,2560]{1,0:T(8,128)(2,1)} async-done(((bf16[2048,2560]{1,0:T(8,128)(2,1)}), bf16[512,2560]{1,0:T(8,128)(2,1)}) %reduce-scatter.11.cloned.1.call-update) | async-done | bytes 2621456 | tf_op jit(solution)/shard_map/reduce_scatter | solution.py:242
  478.3 46.5 %all-gather.12.cloned.1.call-done = bf16[2048,8,64]{0,2,1:T(8,128)(2,1)} async-done(((bf16[512,8,64]{0,2,1:T(8,128)(2,1)}), bf16[2048,8,64]{0,2,1:T(8,128)(2,1)}) %all-gather.12.cloned.1.call-update) | async-done | bytes 2097168 | tf_op jit(solution)/shard_map/all_gather | solution.py:128
  524.7 46.7 %all-gather.10.cloned.1.call-done = bf16[2048,8,64]{0,2,1:T(8,128)(2,1)} async-done(((bf16[512,8,64]{0,2,1:T(8,128)(2,1)}), bf16[2048,8,64]{0,2,1:T(8,128)(2,1)}) %all-gather.10.cloned.1.call-update) | async-done | bytes 2097168 | tf_op jit(solution)/shard_map/all_gather | solution.py:127
  571.6 32.5 %while.32 = (s32[]{:T(128)}, f32[8,512]{1,0:T(8,128)S(1)}, f32[8,512]{1,0:T(8,128)S(1)}, f32[8,512,64]{1,2,0:T(8,128)S(1)}, s32[4]{0:T(128)S(1)}, /*index=5*/s32...) while((s32[]{:T(128)}, f32[8,512]{1,0:T(8,128)S(1)}, ...), condition=%wide.region_18.19_spmd.clone, body=%wide.region_10.18_spmd.clone.sunk | while | flops 561260032 | bytes 30167540 | solution.py:206
  577.5 8.8 conditional.6
  614.3 41.4 %while.33 = (s32[]{:T(128)}, f32[512,8,64]{0,2,1:T(8,128)S(1)}, f32[2048,8,64]{0,2,1:T(8,128)}, f32[2048,8,64]{0,2,1:T(8,128)}, s32[4]{0:T(128)S(1)}, /*index=5*...) while((s32[]{:T(128)}, f32[512,8,64]{0,2,1:T(8,128)S(1)}, ...), condition=%wide.region_28.29_spmd.clone, body=%wide.region_22.28_spmd.clone.sunk | while | flops 1365247488 | bytes 48566832 | solution.py:320
  620.5 17.5 %conditional.7 = ((f32[512,8,64]{0,2,1:T(8,128)S(1)}, f32[2048,8,64]{0,2,1:T(8,128)}, f32[2048,8,64]{0,2,1:T(8,128)})) conditional(s32[]{:T(128)} %convert_element_type.275, (f32[512,8,64]{0,2,1:T(8,128)S(1)}, f32[2048,8,64]{0,2,1:T(8,128)}, f32[2048,8,64]{0,2,1:T(8,128)}) %tuple.111, (s32[]{:T(128)}, bf16[2048,8,64]{0,2,1:T(8,128)(2,1)}, ...), branch_computations={%region_26.26_spmd, %region_27.27_spmd} | conditional | flops 1365245952 | bytes 48562284 | solution.py:318
  624.0 4.1 fusion.16
  628.0 4.5 fusion.34
  667.5 12.4 fusion.52
  680.0 101.0 %reduce-scatter.13.cloned.1.call-done = bf16[512,512]{0,1:T(8,128)(2,1)} async-done(((bf16[2048,512]{0,1:T(8,128)(2,1)}), bf16[512,512]{0,1:T(8,128)(2,1)}) %reduce-scatter.13.cloned.1.call-update) | async-done | bytes 524304 | tf_op jit(solution)/shard_map/reduce_scatter | solution.py:335
  783.9 43.2 %reduce-scatter.15.cloned.1.call-done = bf16[512,512]{1,0:T(8,128)(2,1)} async-done(((bf16[2048,512]{1,0:T(8,128)(2,1)}), bf16[512,512]{1,0:T(8,128)(2,1)}) %reduce-scatter.15.cloned.1.call-update) | async-done | bytes 524304 | tf_op jit(solution)/shard_map/reduce_scatter | solution.py:341
  831.1 5.9 multiply_convert_fusion
  837.0 11.6 reduce-scatter.17.cloned.1.call-start
  848.6 233.8 %all-gather.20.cloned.1.call-done = bf16[2048,3584]{1,0:T(8,128)(2,1)} async-done(((bf16[512,3584]{1,0:T(8,128)(2,1)}), bf16[2048,3584]{1,0:T(8,128)(2,1)}) %all-gather.20.cloned.1.call-update) | async-done | bytes 14680080 | tf_op jit(solution)/shard_map/all_gather | solution.py:357
  1082.4 8.5 convolution_convert_fusion.4
  1091.0 37.6 %all-gather.14.cloned.1.call-done = bf16[2048,512]{1,0:T(8,128)(2,1)} async-done(((bf16[512,512]{1,0:T(8,128)(2,1)}), bf16[2048,512]{1,0:T(8,128)(2,1)}) %all-gather.14.cloned.1.call-update) | async-done | bytes 2097168 | tf_op jit(solution)/shard_map/all_gather | solution.py:220
  1131.7 147.4 %all-gather.16.cloned.1.call-done = bf16[2048,2048]{1,0:T(8,128)(2,1)} async-done(((bf16[512,2048]{1,0:T(8,128)(2,1)}), bf16[2048,2048]{1,0:T(8,128)(2,1)}) %all-gather.16.cloned.1.call-update) | async-done | bytes 8388624 | tf_op jit(solution)/shard_map/all_gather | solution.py:221
  1279.1 8.3 constant_dynamic-update-slice_fusion
  1287.4 8.0 convolution_convert_fusion.5
  1295.5 8.0 convolution_convert_fusion.3
  1303.6 10.3 convolution_convert_fusion.2
  1314.3 8.4 reduce_sum.104
  1322.6 10.9 all-reduce.9
  1337.1 12.5 all-reduce.6
  1349.6 8.5 all-reduce.7
  1360.9 40.0 %all-reduce.13.cloned.1.call-done = (bf16[256,3584]{1,0:T(8,128)(2,1)}, bf16[2560,256]{1,0:T(8,128)(2,1)}) async-done(((bf16[256,3584]{1,0:T(8,128)(2,1)}, bf16[2560,256]{1,0:T(8,128)(2,1)}), (bf16[256,3584]{1,0:T(8,128)(2,1)}, bf16[2560,256]{1,0:T(8,128)(2,1)})) %all-reduce.13.cloned.1.call-update) | async-done | bytes 3145744 | tf_op jit(solution)/shard_map/psum | solution.py:379
  (196 shorter events, 103.9 us)
Async XLA Ops:
  7.2 26.2 %copy-start.10 = (bf16[256,2048]{1,0:T(8,128)(2,1)S(1)}, bf16[256,2048]{1,0:T(8,128)(2,1)}, u32[]{:S(2)}) copy-start(bf16[256,2048]{1,0:T(8,128)(2,1)} %param.27) | copy-start | bytes 3145732
  7.2 26.2 %all-gather.8.cloned.1.call-start = ((), (), s32[]{:S(2)}) async-start(), calls=%async_computation.6 | async-start | bytes 1572864 | tf_op jit(solution)/shard_map/all_gather | solution.py:89
  8.0 20.2 %copy-start.19 = (f32[256]{0:T(256)}, f32[256]{0:T(256)S(1)}, u32[]{:S(2)}) copy-start(f32[256]{0:T(256)S(1)} %convert_element_type.154) | copy-start | bytes 3076
  23.8 4.4 copy-start.15
  26.0 19.2 %all-gather.18.cloned.1.call-start = ((), (), s32[]{:S(2)}) async-start(), calls=%async_computation.13 | async-start | bytes 1572864 | tf_op jit(solution)/shard_map/all_gather | solution.py:237
  26.7 267.7 %reduce-scatter.7.cloned.1.call-start = ((), (), s32[]{:S(2)}) async-start(), calls=%async_computation.7 | async-start | bytes 18350080 | tf_op jit(solution)/shard_map/reduce_scatter | solution.py:95
  28.5 13.5 copy-start.5
  42.0 433.7 %reduce-scatter.11.cloned.1.call-start = ((), (), s32[]{:S(2)}) async-start(), calls=%async_computation.14 | async-start | bytes 13107200 | tf_op jit(solution)/shard_map/reduce_scatter | solution.py:242
  43.5 8.4 copy-start.7
  51.9 472.8 %all-gather.12.cloned.1.call-start = ((), (), s32[]{:S(2)}) async-start(), calls=%async_computation.9 | async-start | bytes 2621440 | tf_op jit(solution)/shard_map/all_gather | solution.py:128
  52.6 249.0 %copy-start.13 = (s32[1,2048]{1,0:T(1,128)S(1)}, s32[1,2048]{1,0:T(1,128)}, u32[]{:S(2)}) copy-start(s32[1,2048]{1,0:T(1,128)} %param.21) | copy-start | bytes 24580
  301.5 269.9 %all-gather.10.cloned.1.call-start = ((), (), s32[]{:S(2)}) async-start(), calls=%async_computation.8 | async-start | bytes 2621440 | tf_op jit(solution)/shard_map/all_gather | solution.py:127
  308.7 472.3 %reduce-scatter.13.cloned.1.call-start = ((), (), s32[]{:S(2)}) async-start(), calls=%async_computation.15 | async-start | bytes 2621440 | tf_op jit(solution)/shard_map/reduce_scatter | solution.py:335
  659.7 167.5 %reduce-scatter.15.cloned.1.call-start = ((), (), s32[]{:S(2)}) async-start(), calls=%async_computation.16 | async-start | bytes 2621440 | tf_op jit(solution)/shard_map/reduce_scatter | solution.py:341
  667.5 414.9 %all-gather.20.cloned.1.call-start = ((), (), s32[]{:S(2)}) async-start(), calls=%async_computation.17 | async-start | bytes 18350080 | tf_op jit(solution)/shard_map/all_gather | solution.py:357
  830.4 298.1 %all-gather.14.cloned.1.call-start = ((), (), s32[]{:S(2)}) async-start(), calls=%async_computation.10 | async-start | bytes 2621440 | tf_op jit(solution)/shard_map/all_gather | solution.py:220
  831.0 448.1 %all-gather.16.cloned.1.call-start = ((), (), s32[]{:S(2)}) async-start(), calls=%async_computation.11 | async-start | bytes 10485760 | tf_op jit(solution)/shard_map/all_gather | solution.py:221
  831.1 251.4 %copy-start.6 = (bf16[256,1536]{1,0:T(8,128)(2,1)S(1)}, bf16[256,1536]{1,0:T(8,128)(2,1)}, u32[]{:S(2)}) copy-start(bf16[256,1536]{1,0:T(8,128)(2,1)} %copy-done.5) | copy-start | bytes 2359300
  831.1 251.3 %copy-start.11 = (bf16[256,2048]{1,0:T(8,128)(2,1)S(1)}, bf16[256,2048]{1,0:T(8,128)(2,1)}, u32[]{:S(2)}) copy-start(bf16[256,2048]{1,0:T(8,128)(2,1)} %param.27) | copy-start | bytes 3145732
  837.0 498.3 %reduce-scatter.17.cloned.1.call-start = ((), (), s32[]{:S(2)}) async-start(), calls=%async_computation.18 | async-start | bytes 1572864 | tf_op jit(solution)/shard_map/reduce_scatter | solution.py:362
  1090.9 267.2 %reduce-scatter.9.cloned.1.call-start = ((), (), s32[]{:S(2)}) async-start(), calls=%async_computation.12 | async-start | bytes 1572864 | tf_op jit(solution)/shard_map/reduce_scatter | solution.py:226
  1131.7 155.7 %copy-start.8 = (bf16[2560,256]{1,0:T(8,128)(2,1)S(1)}, bf16[2560,256]{1,0:T(8,128)(2,1)}, u32[]{:S(2)}) copy-start(bf16[2560,256]{1,0:T(8,128)(2,1)} %copy-done.7) | copy-start | bytes 3932164
  1287.4 8.1 copy-start.4
  1295.4 8.1 copy-start.3
  1295.4 105.4 %all-reduce.13.cloned.1.call-start = ((), (), s32[]{:S(2)}) async-start(), calls=%async_computation.19 | async-start | bytes 6291456 | tf_op jit(solution)/shard_map/psum | solution.py:379
  1303.6 10.4 copy-start.23
  1314.2 21.1 %copy-start.1 = (bf16[1024,256]{1,0:T(8,128)(2,1)S(1)}, bf16[1024,256]{1,0:T(8,128)(2,1)}, u32[]{:S(2)}) copy-start(bf16[1024,256]{1,0:T(8,128)(2,1)} %param.20) | copy-start | bytes 1572868
  1314.2 21.1 %copy-start.16 = (f32[1024]{0:T(1024)S(1)}, f32[1024]{0:T(1024)}, u32[]{:S(2)}) copy-start(f32[1024]{0:T(1024)} %copy-done.15) | copy-start | bytes 12292
  1314.2 21.1 %copy-start.18 = (f32[1024]{0:T(1024)S(1)}, f32[1024]{0:T(1024)}, u32[]{:S(2)}) copy-start(f32[1024]{0:T(1024)} %copy-done.17) | copy-start | bytes 12292
  1314.2 21.1 %copy-start.20 = (f32[256]{0:T(256)S(1)}, f32[256]{0:T(256)}, u32[]{:S(2)}) copy-start(f32[256]{0:T(256)} %copy-done.19) | copy-start | bytes 3076
  1314.3 43.9 %copy-start.9 = (bf16[1024,256]{1,0:T(8,128)(2,1)S(1)}, bf16[1024,256]{1,0:T(8,128)(2,1)}, u32[]{:S(2)}) copy-start(bf16[1024,256]{1,0:T(8,128)(2,1)} %param.31) | copy-start | bytes 1572868
  1400.8 4.6 copy-start.2
  (6 other events, 11.2 us)
Sparse Core Ops, SparseCore 0:
  26.1 7.2 all-gather.7
  34.9 10.1 all-gather.17
  47.5 246.8 reduce-scatter.6
  296.6 179.0 reduce-scatter.10
  477.7 46.9 all-gather.11
  526.7 44.6 all-gather.9
  659.8 121.1 reduce-scatter.12
  783.9 43.1 reduce-scatter.14
  830.5 251.8 all-gather.19
  1084.4 44.1 all-gather.13
  1130.7 148.3 all-gather.15
  1281.8 6.7 reduce-scatter.16
  1295.6 7.0 reduce-scatter.8
  1314.0 86.7 all-reduce.12
where the time goes:
time: 1420 us
  waiting for transfers between devices  1110 us (78%)
  matrix products  72.5 us (5%)
  other arithmetic  67.9 us (5%)
  local copies, waits for them, and re-layouts  53.2 us (4%)
  blocking collectives  45.6 us (3%)
  loops' own time  38.4 us (3%)
  between operations  14.7 us (1%)
    reduce_scatter x1, waiting for transfers between devices, per_device(): lax.psum_scatter(jnp.dot(slice_rows(gathered_hidden, jnp.int32(0), lax.ax...  242 us
    all_gather x1, waiting for transfers between devices, per_device(): d_first_full = lax.all_gather(d_first, 'row', axis=0, tiled=True)  234 us
    reduce_scatter x1, waiting for transfers between devices, per_device(): lax.psum_scatter(lax.dot_general(slice_rows(grad_full, jnp.int32(0), lax....  166 us
    all_gather x1, waiting for transfers between devices, per_device(): lax.all_gather(activated, 'row', axis=0, tiled=True)  147 us
    reduce_scatter x1, waiting for transfers between devices, per_device(): lax.psum_scatter(d_key_total.reshape(all_rows, head_cols).astype(jnp.bflo...  101 us
    all_gather x1, waiting for transfers between devices, over_keys(): lax.all_gather(key_rows, 'row', axis=0, tiled=True)  46.7 us
    all_gather x1, waiting for transfers between devices, over_keys(): lax.all_gather(value_rows, 'row', axis=0, tiled=True)  46.5 us
    reduce_scatter x1, waiting for transfers between devices, per_device(): lax.psum_scatter(d_value_total.reshape(all_rows, head_cols).astype(jnp.bf...  43.2 us
  transfers between devices with their start and end apart: 14, of which 12 were waited for; matrix products, arithmetic and copies ran while one was open for 9% of the time, Pallas kernels for 0%

commit v1 on v0

--- a/solution.py
+++ b/solution.py
@@ -3,16 +3,319 @@
 import jax
 import jax.numpy as jnp
 from jax import lax
+from jax.experimental import pallas as pl
+from jax.experimental.pallas import tpu as pltpu
 from jax.sharding import PartitionSpec as P
 
 D = 1024
 HD = 64
 ROT = 16
 SEQ_LEN = 2048
-
-
 EPSILON = 1e-05
 MASKED = -1000000000.0
+BF = jnp.bfloat16
+F32 = jnp.float32
+NT = (((1,), (1,)), ((), ()))
+NN = (((1,), (0,)), ((), ()))
+TN = (((0,), (0,)), ((), ()))
+
+
+def dot(a, b, dims=NN):
+    return lax.dot_general(a, b, dims, preferred_element_type=F32)
+
+
+BQ = 512
+BK = 256
+
+
+def lane_mask(head, rows):
+    lane = lax.broadcasted_iota(jnp.int32, (rows, 128), 1)
+    return (lane >= head * HD) & (lane < (head + 1) * HD)
+
+
+def attend_forward_kernel(first_ref, q_ref, k_ref, v_ref, rng_ref, out_ref, raw_ref, lse_ref, vt_ref):
+    vt_ref[...] = v_ref[...].astype(F32).T.astype(BF)
+
+    def q_step(qb, _):
+        q0 = pl.multiple_of(qb * BQ, BQ)
+        qs = q_ref[pl.ds(q0, BQ), :] * BF(1.0 / math.sqrt(HD))
+        heads = [jnp.where(lane_mask(h, BQ), qs, BF(0)) for h in range(2)]
+        start = rng_ref[0:1, pl.ds(q0, BQ)]
+        span = rng_ref[1:2, pl.ds(q0, BQ)]
+
+        def k_step(kb, carry):
+            k0 = pl.multiple_of(kb * BK, BK)
+            kk = k_ref[pl.ds(k0, BK), :]
+            kidx = lax.broadcasted_iota(jnp.int32, (BK, BQ), 0) + k0 - start
+            ok = (kidx >= 0) & (kidx <= span)
+            new = []
+            for h in range(2):
+                m, l, acc = carry[h]
+                s = jnp.where(ok, dot(kk, heads[h], NT), MASKED)
+                m2 = jnp.maximum(m, jnp.max(s, 0, keepdims=True))
+                p = jnp.exp(s - m2)
+                c = jnp.exp(m - m2)
+                l = l * c + jnp.sum(p, 0, keepdims=True)
+                vt = vt_ref[h * HD : (h + 1) * HD, pl.ds(k0, BK)]
+                acc = acc * c + dot(vt, p.astype(BF))
+                new.append((m2, l, acc))
+            return tuple(new)
+
+        init = tuple(
+            (jnp.full((1, BQ), -1e30, F32), jnp.zeros((1, BQ), F32), jnp.zeros((HD, BQ), F32))
+            for _ in range(2)
+        )
+        last = (qb + 1) * (BQ // BK)
+        res = lax.fori_loop(first_ref[qb], last, k_step, init)
+        for h in range(2):
+            m, l, acc = res[h]
+            raw_ref[h * HD : (h + 1) * HD, pl.ds(q0, BQ)] = acc / l
+            lse_ref[h : h + 1, pl.ds(q0, BQ)] = m + jnp.log(l)
+        out_ref[pl.ds(q0, BQ), :] = raw_ref[:, pl.ds(q0, BQ)].T.astype(BF)
+        return 0
+
+    lax.fori_loop(0, SEQ_LEN // BQ, q_step, 0)
+
+
+def vmem():
+    return pl.BlockSpec(memory_space=pltpu.VMEM)
+
+
+def smem():
+    return pl.BlockSpec(memory_space=pltpu.SMEM)
+
+
+def attend_forward(first, q, k, v, rng):
+    n = q.shape[0]
+    return pl.pallas_call(
+        attend_forward_kernel,
+        name="attend_forward",
+        out_shape=(
+            jax.ShapeDtypeStruct((n, 128), BF),
+            jax.ShapeDtypeStruct((128, n), F32),
+            jax.ShapeDtypeStruct((8, n), F32),
+        ),
+        in_specs=[smem()] + [vmem()] * 4,
+        out_specs=(vmem(),) * 3,
+        scratch_shapes=[pltpu.VMEM((128, n), BF)],
+        compiler_params=pltpu.CompilerParams(vmem_limit_bytes=48 * 2**20),
+    )(first, q, k, v, rng)
+
+
+def rope(x, c, s1, s2):
+    return x * c + pltpu.roll(x, 120, 1) * s1 + pltpu.roll(x, 8, 1) * s2
+
+
+def rope_back(g, c, s1, s2):
+    return g * c - pltpu.roll(g, 120, 1) * s1 - pltpu.roll(g, 8, 1) * s2
+
+
+def attend_backward_kernel(
+    last_ref, q_ref, k_ref, v_ref, do_ref, raw_ref, lse_ref, rng_ref, c_ref, s1_ref, s2_ref,
+    out_ref, kt_ref, dqt_ref, delta_ref,
+):
+    n = q_ref.shape[0]
+    kt_ref[...] = k_ref[...].astype(F32).T.astype(BF)
+    dqt_ref[...] = jnp.zeros_like(dqt_ref)
+
+    def delta_step(i, _):
+        at = pl.ds(pl.multiple_of(i * BQ, BQ), BQ)
+        prod = do_ref[at, :].astype(F32).T * raw_ref[:, at]
+        for h in range(2):
+            delta_ref[h : h + 1, at] = jnp.sum(prod[h * HD : (h + 1) * HD], 0, keepdims=True)
+        return 0
+
+    lax.fori_loop(0, n // BQ, delta_step, 0)
+
+    def k_step(kb, _):
+        k0 = pl.multiple_of(kb * BK, BK)
+        kk = k_ref[pl.ds(k0, BK), :]
+        vv = v_ref[pl.ds(k0, BK), :]
+
+        def q_step(qb, carry):
+            dk, dv = carry
+            q0 = pl.multiple_of(qb * BQ, BQ)
+            at = pl.ds(q0, BQ)
+            qs = q_ref[at, :] * BF(1.0 / math.sqrt(HD))
+            do = do_ref[at, :]
+            kidx = lax.broadcasted_iota(jnp.int32, (BK, BQ), 0) + k0 - rng_ref[0:1, at]
+            ok = (kidx >= 0) & (kidx <= rng_ref[1:2, at])
+            for h in range(2):
+                qh = jnp.where(lane_mask(h, BQ), qs, BF(0))
+                doh = jnp.where(lane_mask(h, BQ), do, BF(0))
+                s = jnp.where(ok, dot(kk, qh, NT), MASKED)
+                p = jnp.exp(s - lse_ref[h : h + 1, at])
+                ds = (p * (dot(vv, doh, NT) - delta_ref[h : h + 1, at])).astype(BF)
+                dv = dv + dot(p.astype(BF), doh)
+                dk = dk + dot(ds, qh)
+                rows = slice(h * HD, (h + 1) * HD)
+                dqt_ref[rows, at] += dot(kt_ref[rows, pl.ds(k0, BK)], ds)
+            return dk, dv
+
+        zero = jnp.zeros((BK, 128), F32)
+        dk, dv = lax.fori_loop(k0 // BQ, last_ref[kb], q_step, (zero, zero))
+        at = pl.ds(k0, BK)
+        out_ref[at, 128:256] = rope_back(dk, c_ref[at, :], s1_ref[at, :], s2_ref[at, :]).astype(BF)
+        out_ref[at, 256:384] = dv.astype(BF)
+        return 0
+
+    lax.fori_loop(0, n // BK, k_step, 0)
+
+    def finish(i, _):
+        at = pl.ds(pl.multiple_of(i * BQ, BQ), BQ)
+        dq = dqt_ref[:, at].T * (1.0 / math.sqrt(HD))
+        out_ref[at, 0:128] = rope_back(dq, c_ref[at, :], s1_ref[at, :], s2_ref[at, :]).astype(BF)
+        return 0
+
+    lax.fori_loop(0, n // BQ, finish, 0)
+
+
+def attend_backward(last, q, k, v, do, raw, lse, rng, c, s1, s2):
+    n = q.shape[0]
+    return pl.pallas_call(
+        attend_backward_kernel,
+        name="attend_backward",
+        out_shape=jax.ShapeDtypeStruct((n, 384), BF),
+        in_specs=[smem()] + [vmem()] * 10,
+        out_specs=vmem(),
+        scratch_shapes=[
+            pltpu.VMEM((128, n), BF),
+            pltpu.VMEM((128, n), F32),
+            pltpu.VMEM((8, n), F32),
+        ],
+        compiler_params=pltpu.CompilerParams(vmem_limit_bytes=56 * 2**20),
+    )(last, q, k, v, do, raw, lse, rng, c, s1, s2)
+
+
+def rope_tables(pos):
+    half = ROT // 2
+    freq = 10000.0 ** (-(jnp.arange(half, dtype=F32) * 2.0 / ROT))
+    ang = pos.astype(F32)[None, :] * freq[:, None]
+    cs, sn = lax.optimization_barrier((jnp.cos(ang), jnp.sin(ang)))
+    cs, sn = cs.T, sn.T
+    n = pos.shape[0]
+    one = jnp.ones((n, HD - ROT), F32)
+    zero = jnp.zeros((n, HD - ROT), F32)
+    z8 = jnp.zeros((n, half), F32)
+    c = jnp.concatenate([cs, cs, one] * 2, 1)
+    s1 = jnp.concatenate([-sn, z8, zero] * 2, 1)
+    s2 = jnp.concatenate([z8, sn, zero] * 2, 1)
+    return c, s1, s2
+
+
+def per_device_sliced(
+    inputs, segments, ln_gain, ln_bias, w_qkv, b_qkv, w_out, w_up, b_up, w_down, out_bias, cotangent
+):
+    nrow = lax.axis_size("row")
+    row = lax.axis_index("row")
+    dpart = inputs.shape[1]
+    hcols = w_qkv.shape[2] // nrow
+    fcols = w_up.shape[1] // nrow
+    toks = segments.shape[1]
+    half = inputs.shape[0]
+
+    seg = segments[0]
+    idx = jnp.arange(toks, dtype=jnp.int32)
+    start = jnp.sum(
+        jnp.where(seg[None, :] < seg[:, None], 1, 0), 1, dtype=jnp.int32
+    )
+    pos = idx - start
+    c, s1, s2 = rope_tables(pos)
+    rng = jnp.concatenate([start[None], pos[None], jnp.zeros((6, toks), jnp.int32)], 0)
+    first = start[::BQ] // BK
+    ends = jnp.sum(jnp.where(start[None, :] <= idx[BK - 1 :: BK, None], 1, 0), 1, dtype=jnp.int32)
+    last = (ends + BQ - 1) // BQ
+
+    xg = lax.all_gather(lax.all_gather(inputs, "row"), "col", axis=1, tiled=True)
+    cg = lax.all_gather(lax.all_gather(cotangent, "row"), "col", axis=1, tiled=True)
+    gb = lax.all_gather(jnp.stack([ln_gain, ln_bias]).astype(F32), "row")
+    w1s = jnp.concatenate(
+        [
+            w_qkv.reshape(dpart, 3, nrow, hcols).transpose(2, 0, 1, 3).reshape(nrow, dpart, 3 * hcols),
+            w_up.reshape(dpart, nrow, fcols).transpose(1, 0, 2),
+        ],
+        2,
+    )
+    w2s = jnp.concatenate(
+        [w_out.reshape(nrow, hcols, dpart), w_down.reshape(nrow, fcols, dpart)], 1
+    )
+    w1 = lax.all_to_all(w1s, "row", 0, 0)
+    w2 = lax.all_to_all(w2s, "row", 0, 0)
+    b1 = jnp.concatenate(
+        [
+            lax.dynamic_slice_in_dim(b_qkv, row * hcols, hcols, 1).reshape(-1),
+            lax.dynamic_slice_in_dim(b_up, row * fcols, fcols, 0),
+        ]
+    ).astype(F32)
+
+    xf = xg.astype(F32)
+    mean = jnp.sum(xf, (0, 2)) / D
+    var = jnp.sum(xf * xf, (0, 2)) / D - mean * mean
+    inv = lax.rsqrt(var + EPSILON)
+    xhat = (xf - mean[None, :, None]) * inv[None, :, None]
+    normed = (xhat * gb[:, 0:1] + gb[:, 1:2]).astype(BF)
+    nd = normed.transpose(1, 0, 2).reshape(toks, D)
+    proj = dot(nd, w1.reshape(D, -1)) + b1
+    h3 = 3 * hcols
+
+    def rp(x):
+        return (
+            x * c + jnp.roll(x, -8, 1) * s1 + jnp.roll(x, 8, 1) * s2
+        ).astype(BF)
+
+    q, k, v = rp(proj[:, :hcols]), rp(proj[:, hcols : 2 * hcols]), proj[:, 2 * hcols : h3].astype(BF)
+    up = proj[:, h3:]
+    phi = 0.5 * (1.0 + lax.erf(up * (1.0 / math.sqrt(2.0))))
+    act = (up * phi).astype(BF)
+    gp = phi + up * jnp.exp(-0.5 * up * up) * (1.0 / math.sqrt(2.0 * math.pi))
+    attended, raw, lse = attend_forward(first, q, k, v, rng)
+
+    joined = jnp.concatenate([attended, act], 1)
+    col = lax.axis_index("col")
+    outp = jnp.einsum("tk,bkn->btn", joined, w2, preferred_element_type=F32).astype(BF)
+    outp = lax.psum_scatter(outp, "row", scatter_dimension=0)
+    outp = lax.psum_scatter(outp, "col", scatter_dimension=0, tiled=True)
+    layer_out = (inputs.astype(F32) + outp.astype(F32) + out_bias.astype(F32)).astype(BF)
+    gob = jnp.sum(cotangent.astype(F32), 0)
+    cgd = cg.transpose(1, 0, 2).reshape(toks, D)
+    w2d = w2.transpose(1, 0, 2).reshape(-1, D)
+    g2 = dot(joined, cgd, TN)
+    dj = dot(cgd, w2d, NT)
+    datt = dj[:, :hcols].astype(BF)
+    dup = (dj[:, hcols:] * gp).astype(BF)
+    dproj = attend_backward(last, q, k, v, datt, raw, lse, rng, c, s1, s2)
+    d1 = jnp.concatenate([dproj, dup], 1)
+    g1 = dot(nd, d1, TN)
+    gb1 = jnp.sum(d1.astype(F32), 0)
+    dn = jnp.einsum("tn,bkn->btk", d1, w1, preferred_element_type=F32).astype(BF)
+    dn = lax.psum_scatter(dn, "row", scatter_dimension=0)
+    dn = lax.psum_scatter(dn, "col", scatter_dimension=0, tiled=True).astype(F32)
+    myx = lax.dynamic_slice_in_dim(mean, col * half, half), lax.dynamic_slice_in_dim(inv, col * half, half)
+    xh = (inputs.astype(F32) - myx[0][:, None]) * myx[1][:, None]
+    dc = dn * ln_gain.astype(F32)
+    st = lax.psum((jnp.sum(dc, 1), jnp.sum(dc * xh, 1)), "row")
+    grad_inputs = myx[1][:, None] * (
+        dc - st[0][:, None] / D - xh * st[1][:, None] / D
+    ) + cotangent.astype(F32)
+    ng = lax.psum((jnp.sum(dn * xh, 0), jnp.sum(dn, 0), gob), ("dp", "col"))
+
+    g1 = lax.psum(g1.astype(BF), "dp").reshape(nrow, dpart, -1)
+    g2 = lax.psum(g2.astype(BF), "dp").reshape(-1, nrow, dpart).transpose(1, 0, 2)
+    g1 = lax.all_to_all(g1, "row", 0, 0).astype(F32)
+    g2 = lax.all_to_all(g2, "row", 0, 0).astype(F32)
+    gb1 = lax.all_gather(lax.psum(gb1, "dp"), "row")
+    grad_w_qkv = g1[:, :, :h3].reshape(nrow, dpart, 3, hcols).transpose(1, 2, 0, 3).reshape(dpart, 3, -1)
+    grad_w_up = g1[:, :, h3:].transpose(1, 0, 2).reshape(dpart, -1)
+    grad_w_out = g2[:, :hcols].reshape(-1, dpart)
+    grad_w_down = g2[:, hcols:].reshape(-1, dpart)
+    grad_b_qkv = gb1[:, :h3].reshape(nrow, 3, hcols).transpose(1, 0, 2).reshape(3, -1)
+    grad_b_up = gb1[:, h3:].reshape(-1)
+    return (
+        layer_out, grad_inputs, ng[0], ng[1], grad_w_qkv, grad_b_qkv,
+        grad_w_out, grad_w_up, grad_b_up, grad_w_down, ng[2],
+    )
+
+
 FLOOR_INIT = -1e30
 
 
@@ -58,7 +361,7 @@
     return (q_list, k_list)
 
 
-def per_device(
+def per_device_general(
     inputs, segments, ln_gain, ln_bias, w_qkv, b_qkv, w_out, w_up, b_up, w_down, out_bias, cotangent
 ):
     local_rows, feature_cols = inputs.shape
@@ -418,8 +721,10 @@
         P("row"),
         P(("dp", "col"), "row"),
     )
+    size = dict(mesh.shape)
+    sliced = (size["dp"], size["row"], size["col"]) == (4, 4, 2)
     return jax.shard_map(
-        per_device,
+        per_device_sliced if sliced else per_device_general,
         mesh=mesh,
         in_specs=placed,
         out_specs=(

time: 1420 us -> 678 us (0.48)
  waiting for transfers between devices: 1110 us -> 341 us
  blocking collectives: 45.6 us -> 108 us
  Pallas kernels: 0 us -> 55.5 us
  loops' own time: 38.4 us -> 0 us
  other arithmetic: 67.9 us -> 31.9 us
  matrix products: 72.5 us -> 38.2 us
    all_gather x7 -> x4, waiting for transfers between devices: 518 us -> 54.2 us  [the longest x1 49.5 us: per_device_sliced(): lax.all_gather(inputs, 'row')]
    reduce_scatter x6 -> x4, waiting for transfers between devices: 552 us -> 199 us  [the longest x1 105 us: per_device_sliced(): outp = lax.psum_scatter(outp, 'row', scatter_dimension=0)]
    all_gather x0 -> x2, blocking collectives: none -> 77 us  [the longest x1 58.3 us: per_device_sliced(): gb = lax.all_gather(jnp.stack([ln_gain, ln_bias]).astype(F32), 'row')]
    pallas_call x0 -> x2, Pallas kernels: none -> 55.5 us  [the longest x1 36 us: attend_backward(): pl.pallas_call(attend_backward_kernel, name='attend_backward', out_shape=...]
    another operation x10 -> x0, loops' own time: 38.4 us -> none  [the longest x1 18.6 us: backward_piece(): lax.scan(backward_pair_step, (d_query_acc, zero_keys, zero_keys), (q_list...]
    dot_general x13 -> x6, matrix products: 72.5 us -> 38.2 us  [the longest x4 23.3 us: dot(): return lax.dot_general(a, b, dims, preferred_element_type=F32)]
    psum x1, waiting for transfers between devices: 40 us -> 69.2 us  [per_device_sliced(): g1 = lax.psum(g1.astype(BF), 'dp').reshape(nrow, dpart, -1)]
    all_to_all x0 -> x4, starting transfers between devices: none -> 22.2 us  [the longest x1 8.36 us: per_device_sliced(): g1 = lax.all_to_all(g1, 'row', 0, 0).astype(F32)]
  transfers between devices with their start and end apart: 14 -> 13, of which waited for: 12 -> 6; matrix products, arithmetic and copies ran while one was open for 9% -> 12% of each run, Pallas kernels for 0% -> 0%
where the time goes in v1:
time: 678 us; the launch traced here: 674 us
  waiting for transfers between devices  341 us (50%)
  blocking collectives  108 us (16%)
  local copies, waits for them, and re-layouts  61.9 us (9%)
  Pallas kernels  55.5 us (8%)
  matrix products  38.2 us (6%)
  other arithmetic  31.9 us (5%)
  starting transfers between devices  22.4 us (3%)
  between operations  14.5 us (2%)
    reduce_scatter x1, waiting for transfers between devices, per_device_sliced(): outp = lax.psum_scatter(outp, 'row', scatter_dimension=0)  105 us
    reduce_scatter x1, waiting for transfers between devices, per_device_sliced(): dn = lax.psum_scatter(dn, 'row', scatter_dimension=0)  93.6 us
    psum x1, waiting for transfers between devices, per_device_sliced(): g1 = lax.psum(g1.astype(BF), 'dp').reshape(nrow, dpart, -1)  69.2 us
    all_gather x1, blocking collectives, per_device_sliced(): gb = lax.all_gather(jnp.stack([ln_gain, ln_bias]).astype(F32), 'row')  58.3 us
    all_gather x1, waiting for transfers between devices, per_device_sliced(): lax.all_gather(inputs, 'row')  49.5 us
    pallas_call x1, Pallas kernels, attend_backward(): pl.pallas_call(attend_backward_kernel, name='attend_backward', out_shape=...  36 us
    dot_general x4, matrix products, dot(): return lax.dot_general(a, b, dims, preferred_element_type=F32)  23.3 us
    pallas_call x1, Pallas kernels, attend_forward(): pl.pallas_call(attend_forward_kernel, name='attend_forward', out_shape=(j...  19.5 us
  transfers between devices with their start and end apart: 13, of which 6 were waited for; matrix products, arithmetic and copies ran while one was open for 12% of the time, Pallas kernels for 0%

profile of v1, /device:TPU:0, one launch (start us, length us, event | category | flops | bytes accessed | tf_op | source)
XLA Modules:
  0.0 673.6 jit_solution(12473150756082535073)
XLA Ops:
  8.7 49.5 %all-gather.12.cloned.1.call-done = bf16[4096,256]{1,0:T(8,128)(2,1)} async-done(((bf16[1024,256]{1,0:T(8,128)(2,1)}), bf16[4096,256]{1,0:T(8,128)(2,1)}) %all-gather.12.cloned.1.call-update) | async-done | bytes 2097168 | tf_op jit(solution)/shard_map/all_gather | solution.py:229
  62.6 4.4 all-to-all-start.1
  69.1 3.7 multiply_sine_fusion
  74.2 4.4 concatenate.60.s1_ref
  78.7 4.4 concatenate.62.s2_ref
  89.7 58.3 %all_gather.31 = f32[4,2,256]{2,1,0:T(2,128)S(1)} all-gather(f32[1,2,256]{2,1,0:T(2,128)S(1)} %maximum_convert_fusion.1), channel_id=1, replica_groups=mesh['dp'=4,'row'=4,'col'=2] {'row'}, dimensions={0}, use_global_device_ids=true | all-gather | bytes 10240 | tf_op jit(solution)/shard_map/all_gather | solution.py:231
  150.1 4.6 all-gather.8.cloned.1.call-done
  154.7 3.6 convert_reduce_fusion
  158.3 3.0 fusion.11
  161.3 4.8 all-to-all-start
  166.1 7.6 %bitcast_add_fusion = f32[2048,896]{1,0:T(8,128)S(1)} fusion(bf16[2048,4,256]{2,0,1:T(8,128)(2,1)} %fusion.11, bf16[4,256,896]{1,2,0:T(8,128)(2,1)} %all-to-all-done.1, f32[896]{0:T(1024)S(1)} %maximum_convert_fusion), kind=kOutput, calls=%fused_computation.9 | convolution fusion | flops 3759931392 | bytes 13372928 | tf_op jit(solution)/shard_map/dot_general | solution.py:24
  180.6 17.4 %all-to-all-done = bf16[4,640,256]{1,2,0:T(8,128)(2,1)S(1)} async-done(((bf16[4,640,256]{1,2,0:T(8,128)(2,1)}), bf16[4,640,256]{1,2,0:T(8,128)(2,1)S(1)}, u32[]{:S(2)}, u32[]{:S(2)}) %all-to-all-start) | async-done | bytes 1310752 | tf_op jit(solution)/shard_map/all_to_all | solution.py:243
  197.9 5.7 convolution_bitcast_fusion
  203.7 3.5 fusion.10
  208.1 6.4 copy.124
  214.4 6.4 copy.127
  220.9 5.6 fusion.31
  226.6 19.5 %attend_forward.1 = (bf16[2048,128]{1,0:T(8,128)(2,1)S(1)}, f32[128,2048]{1,0:T(8,128)S(1)}, f32[8,2048]{1,0:T(8,128)S(1)}) custom-call(s32[4]{0:T(128)S(1)} %and_select_fusion.1.first_ref, bf16[2048,128]{1,0:T(8,128)(2,1)S(1)} %get-tuple-element.101.q_ref, bf16[2048,128]{1,0:T(8,128)(2,1)S(1)} %get-tuple-element.100.k_ref, ...), custom_call_target="tpu_custom_call" | custom-call | tf_op jit(solution)/shard_map/attend_forward/pallas_call | solution.py:90
  250.3 36.0 %attend_backward.1 = bf16[2048,384]{1,0:T(8,128)(2,1)} custom-call(s32[8]{0:T(128)} %and_select_fusion.last_ref, bf16[2048,128]{1,0:T(8,128)(2,1)} %copy-done.3, bf16[2048,128]{1,0:T(8,128)(2,1)} %copy-done.2, bf16[2048,128]{1,0:T(8,128)(2,1)} %copy-done.4, bf16[2048,128]{1,0:T(8,128)(2,1)} %slice.158.do_ref, f32[128,2048]{1,0:T(8,128)} %copy-done.5, ...), custom_call_target="tpu_custom_call" | custom-call | tf_op jit(solution)/shard_map/attend_backward/pallas_call | solution.py:175
  286.3 7.1 %convolution_convert_fusion = bf16[1024,896]{1,0:T(8,128)(2,1)} fusion(bf16[2048,1024]{0,1:T(8,128)(2,1)S(1)} %bitcast.101, bf16[2048,512]{1,0:T(8,128)(2,1)S(1)} %copy-done.14, bf16[2048,384]{1,0:T(8,128)(2,1)} %attend_backward.1), kind=kOutput, calls=%fused_computation.29 | convolution fusion | flops 3766353920 | bytes 9699328 | tf_op jit(solution)/shard_map/dot_general | solution.py:24
  293.5 3.6 copy.125
  297.1 8.5 %convert_bitcast_fusion = bf16[4,2048,256]{1,2,0:T(8,128)(2,1)} fusion(bf16[4,256,896]{1,2,0:T(8,128)(2,1)} %all-to-all-done.1, bf16[2048,512]{1,0:T(8,128)(2,1)S(1)} %copy-done.14, bf16[2048,384]{1,0:T(8,128)(2,1)} %attend_backward.1), kind=kOutput, calls=%fused_computation.19 | convolution fusion | flops 3767533568 | bytes 9699328 | tf_op jit(solution)/shard_map/tn,bkn->btk/dot_general | solution.py:290
  307.1 6.4 convert_bitcast_fusion.1
  313.6 69.2 %all-reduce.5.cloned.1.call-done = (bf16[4,256,896]{1,2,0:T(8,128)(2,1)}, bf16[4,640,256]{2,1,0:T(8,128)(2,1)}) async-done(((bf16[4,256,896]{1,2,0:T(8,128)(2,1)}, bf16[4,640,256]{2,1,0:T(8,128)(2,1)}), (bf16[4,256,896]{1,2,0:T(8,128)(2,1)}, bf16[4,640,256]{2,1,0:T(8,128)(2,1)})) %all-reduce.5.cloned.1.call-update) | async-done | bytes 3145744 | tf_op jit(solution)/shard_map/psum | solution.py:302
  382.7 4.6 all-to-all-start.3
  387.3 93.6 %reduce-scatter.9.cloned.1.call-done = bf16[1,2048,256]{1,2,0:T(8,128)(2,1)} async-done(((bf16[4,2048,256]{1,2,0:T(8,128)(2,1)}), bf16[1,2048,256]{1,2,0:T(8,128)(2,1)}) %reduce-scatter.9.cloned.1.call-update) | async-done | bytes 1048592 | tf_op jit(solution)/shard_map/reduce_scatter | solution.py:291
  481.0 8.4 %all-to-all-start.2 = ((bf16[4,256,896]{1,2,0:T(8,128)(2,1)}), bf16[4,256,896]{1,2,0:T(8,128)(2,1)S(1)}, u32[]{:S(2)}, u32[]{:S(2)}) async-start(bf16[4,256,896]{1,2,0:T(8,128)(2,1)} %get-tuple-element.98), calls=%async_computation.6 | async-start | bytes 3670016 | tf_op jit(solution)/shard_map/all_to_all | solution.py:304
  489.4 105.1 %reduce-scatter.5.cloned.1.call-done = bf16[1,2048,256]{1,2,0:T(8,128)(2,1)} async-done(((bf16[4,2048,256]{1,2,0:T(8,128)(2,1)}), bf16[1,2048,256]{1,2,0:T(8,128)(2,1)}) %reduce-scatter.5.cloned.1.call-update) | async-done | bytes 1048592 | tf_op jit(solution)/shard_map/reduce_scatter | solution.py:276
  601.2 8.9 %psum.61 = f32[1,896]{1,0:T(1,128)S(1)} all-reduce(f32[1,896]{1,0:T(1,128)S(1)} %all_gather.35), channel_id=1, replica_groups=mesh['dp'=4,'row'=4,'col'=2] {'dp'}, use_global_device_ids=true, to_apply=%region_18.19 | all-reduce | flops 896 | bytes 7168 | tf_op jit(solution)/shard_map/psum | solution.py:306
  610.2 18.7 %all-gather.2 = f32[4,1,896]{2,1,0:T(1,128)S(1)} all-gather(f32[1,1,896]{2,1,0:T(1,128)S(1)} %bitcast.118), channel_id=1, replica_groups=mesh['dp'=4,'row'=4,'col'=2] {'row'}, dimensions={0}, use_global_device_ids=true | all-gather | bytes 17920 | tf_op jit(solution)/shard_map/all_gather | solution.py:306
  640.2 10.0 %all-reduce.1 = (f32[1024]{0:T(1024)S(1)}, f32[1024]{0:T(1024)S(1)}) all-reduce(f32[1024]{0:T(1024)S(1)} %get-tuple-element.90, f32[1024]{0:T(1024)S(1)} %get-tuple-element.91), channel_id=1, replica_groups=mesh['dp'=4,'row'=4,'col'=2] {'row'}, use_global_device_ids=true, to_apply=%region_11.12 | all-reduce | flops 2048 | bytes 16384 | tf_op jit(solution)/shard_map/psum | solution.py:296
  654.5 12.3 %all-reduce = (f32[256]{0:T(256)}, f32[256]{0:T(256)}, f32[256]{0:T(256)}) all-reduce(f32[256]{0:T(256)S(1)} %get-tuple-element.89, f32[256]{0:T(256)S(1)} %get-tuple-element.92, f32[256]{0:T(256)S(1)} %get-tuple-element.112), channel_id=1, replica_groups=mesh['dp'=4,'row'=4,'col'=2] {'dp','col'}, use_global_device_ids=true, to_apply=%region_13.14 | all-reduce | flops 768 | bytes 6144 | tf_op jit(solution)/shard_map/psum | solution.py:300
  (144 shorter events, 53.8 us)
Async XLA Ops:
  7.2 140.8 %copy-start = (bf16[3,512]{1,0:T(4,128)(2,1)S(1)}, bf16[3,512]{1,0:T(4,128)(2,1)}, u32[]{:S(2)}) copy-start(bf16[3,512]{1,0:T(4,128)(2,1)} %param.17) | copy-start | bytes 9220
  7.2 53.5 %copy-start.22 = (bf16[256,2048]{1,0:T(8,128)(2,1)S(1)}, bf16[256,2048]{1,0:T(8,128)(2,1)}, u32[]{:S(2)}) copy-start(bf16[256,2048]{1,0:T(8,128)(2,1)} %param.19) | copy-start | bytes 3145732
  7.2 51.1 %all-gather.12.cloned.1.call-start = ((), (), s32[]{:S(2)}) async-start(), calls=%async_computation.14 | async-start | bytes 2621440 | tf_op jit(solution)/shard_map/all_gather | solution.py:229
  7.9 142.0 %all-gather.14.cloned.1.call-start = ((), (), s32[]{:S(2)}) async-start(), calls=%async_computation.15 | async-start | bytes 2621440 | tf_op jit(solution)/shard_map/all_gather | solution.py:230
  8.7 146.0 %all-gather.8.cloned.1.call-start = ((), (), s32[]{:S(2)}) async-start(), calls=%async_computation.8 | async-start | bytes 6291456 | tf_op jit(solution)/shard_map/all_gather | solution.py:229
  61.2 5.9 copy-start.24
  61.3 5.9 copy-start.25
  61.3 5.9 copy-start.23
  62.6 98.7 %all-to-all-start.1 = ((bf16[4,256,896]{1,2,0:T(8,128)(2,1)}), bf16[4,256,896]{1,2,0:T(8,128)(2,1)}, u32[]{:S(2)}, u32[]{:S(2)}) async-start(bf16[4,256,896]{1,2,0:T(8,128)(2,1)} %pad_maximum_fusion.2), calls=%async_computation.1 | async-start | bytes 3670016 | tf_op jit(solution)/shard_map/all_to_all | solution.py:242
  67.1 130.9 %all-gather.10.cloned.1.call-start = ((), (), s32[]{:S(2)}) async-start(), calls=%async_computation.11 | async-start | bytes 6291456 | tf_op jit(solution)/shard_map/all_gather | solution.py:230
  150.1 76.5 %copy-start.6 = (s32[8,2048]{1,0:T(8,128)}, s32[8,2048]{1,0:T(8,128)S(1)}, u32[]{:S(2)}) copy-start(s32[8,2048]{1,0:T(8,128)S(1)} %add_add_fusion.rng_ref) | copy-start | bytes 196612
  161.3 36.6 %all-to-all-start = ((bf16[4,640,256]{1,2,0:T(8,128)(2,1)}), bf16[4,640,256]{1,2,0:T(8,128)(2,1)S(1)}, u32[]{:S(2)}, u32[]{:S(2)}) async-start(bf16[4,640,256]{1,2,0:T(8,128)(2,1)} %pad_maximum_fusion.7), calls=%async_computation | async-start | bytes 2621440 | tf_op jit(solution)/shard_map/all_to_all | solution.py:243
  166.1 216.6 %all-reduce.5.cloned.1.call-start = ((), (), s32[]{:S(2)}) async-start(), calls=%async_computation.16 | async-start | bytes 6291456 | tf_op jit(solution)/shard_map/psum | solution.py:302
  173.8 52.9 %copy-start.4 = (bf16[2048,128]{1,0:T(8,128)(2,1)}, bf16[2048,128]{1,0:T(8,128)(2,1)S(1)}, u32[]{:S(2)}) copy-start(bf16[2048,128]{1,0:T(8,128)(2,1)S(1)} %slice.159.v_ref) | copy-start | bytes 1572868
  197.9 5.8 copy-start.9
  214.4 6.5 copy-start.12
  214.4 6.5 copy-start.13
  220.9 25.3 %copy-start.17 = (bf16[2048,4,256]{0,2,1:T(8,128)(2,1)S(1)}, bf16[2048,4,256]{0,2,1:T(8,128)(2,1)}, u32[]{:S(2)}) copy-start(bf16[2048,4,256]{0,2,1:T(8,128)(2,1)} %copy.127) | copy-start | bytes 12582916
  220.9 25.3 %copy-start.18 = (bf16[2048,512]{1,0:T(8,128)(2,1)S(1)}, bf16[2048,512]{1,0:T(8,128)(2,1)}, u32[]{:S(2)}) copy-start(bf16[2048,512]{1,0:T(8,128)(2,1)} %get-tuple-element.103) | copy-start | bytes 6291460
  226.6 22.5 %copy-start.2 = (bf16[2048,128]{1,0:T(8,128)(2,1)}, bf16[2048,128]{1,0:T(8,128)(2,1)S(1)}, u32[]{:S(2)}) copy-start(bf16[2048,128]{1,0:T(8,128)(2,1)S(1)} %get-tuple-element.100.k_ref) | copy-start | bytes 1572868
  226.6 22.5 %copy-start.3 = (bf16[2048,128]{1,0:T(8,128)(2,1)}, bf16[2048,128]{1,0:T(8,128)(2,1)S(1)}, u32[]{:S(2)}) copy-start(bf16[2048,128]{1,0:T(8,128)(2,1)S(1)} %get-tuple-element.101.q_ref) | copy-start | bytes 1572868
  250.3 36.0 %copy-start.14 = (bf16[2048,512]{1,0:T(8,128)(2,1)S(1)}, bf16[2048,512]{1,0:T(8,128)(2,1)}, u32[]{:S(2)}) copy-start(bf16[2048,512]{1,0:T(8,128)(2,1)} %get-tuple-element.102) | copy-start | bytes 6291460
  250.3 36.0 %copy-start.16 = (bf16[2048,4,256]{0,2,1:T(8,128)(2,1)S(1)}, bf16[2048,4,256]{0,2,1:T(8,128)(2,1)}, u32[]{:S(2)}) copy-start(bf16[2048,4,256]{0,2,1:T(8,128)(2,1)} %copy.124) | copy-start | bytes 12582916
  297.0 183.9 %reduce-scatter.9.cloned.1.call-start = ((), (), s32[]{:S(2)}) async-start(), calls=%async_computation.12 | async-start | bytes 5242880 | tf_op jit(solution)/shard_map/reduce_scatter | solution.py:291
  305.6 288.9 %reduce-scatter.5.cloned.1.call-start = ((), (), s32[]{:S(2)}) async-start(), calls=%async_computation.9 | async-start | bytes 5242880 | tf_op jit(solution)/shard_map/reduce_scatter | solution.py:276
  382.7 98.2 %all-to-all-start.3 = ((bf16[4,640,256]{2,1,0:T(8,128)(2,1)}), bf16[4,640,256]{2,1,0:T(8,128)(2,1)S(1)}, u32[]{:S(2)}, u32[]{:S(2)}) async-start(bf16[4,640,256]{2,1,0:T(8,128)(2,1)} %get-tuple-element.99), calls=%async_computation.7 | async-start | bytes 2621440 | tf_op jit(solution)/shard_map/all_to_all | solution.py:305
  387.3 211.2 %copy-start.26 = (bf16[256]{0:T(256)(128)(2,1)S(1)}, bf16[256]{0:T(256)(128)(2,1)}, u32[]{:S(2)}) copy-start(bf16[256]{0:T(256)(128)(2,1)} %param.22) | copy-start | bytes 1540
  387.3 251.3 %reduce-scatter.11.cloned.1.call-start = ((), (), s32[]{:S(2)}) async-start(), calls=%async_computation.13 | async-start | bytes 1572864 | tf_op jit(solution)/shard_map/reduce_scatter | solution.py:292
  481.0 151.4 %all-to-all-start.2 = ((bf16[4,256,896]{1,2,0:T(8,128)(2,1)}), bf16[4,256,896]{1,2,0:T(8,128)(2,1)S(1)}, u32[]{:S(2)}, u32[]{:S(2)}) async-start(bf16[4,256,896]{1,2,0:T(8,128)(2,1)} %get-tuple-element.98), calls=%async_computation.6 | async-start | bytes 3670016 | tf_op jit(solution)/shard_map/all_to_all | solution.py:304
  489.4 160.9 %reduce-scatter.7.cloned.1.call-start = ((), (), s32[]{:S(2)}) async-start(), calls=%async_computation.10 | async-start | bytes 1572864 | tf_op jit(solution)/shard_map/reduce_scatter | solution.py:277
  634.3 16.0 %copy-start.20 = (bf16[1024,256]{0,1:T(8,128)(2,1)S(1)}, bf16[1024,256]{0,1:T(8,128)(2,1)}, u32[]{:S(2)}) copy-start(bf16[1024,256]{0,1:T(8,128)(2,1)} %copy.123) | copy-start | bytes 1572868
  635.8 31.1 %copy-start.1 = (bf16[3,512]{1,0:T(4,128)(2,1)S(1)}, bf16[3,512]{1,0:T(4,128)(2,1)}, u32[]{:S(2)}) copy-start(bf16[3,512]{1,0:T(4,128)(2,1)} %param.17) | copy-start | bytes 9220
  (8 other events, 26.9 us)
Sparse Core Ops, SparseCore 0:
  9.6 48.6 all-gather.11
  59.8 80.8 all-gather.13
  142.3 12.3 all-gather.7
  156.1 14.7 all-gather.9
  297.2 85.5 all-reduce.4
  385.0 95.9 reduce-scatter.8
  483.3 111.1 reduce-scatter.4
  596.8 13.1 reduce-scatter.10
  612.2 9.6 reduce-scatter.6

commit v2 on v1

--- a/solution.py
+++ b/solution.py
@@ -106,12 +106,17 @@
     return x * c + pltpu.roll(x, 120, 1) * s1 + pltpu.roll(x, 8, 1) * s2
 
 
-def rope_back(g, c, s1, s2):
-    return g * c - pltpu.roll(g, 120, 1) * s1 - pltpu.roll(g, 8, 1) * s2
+def unrope(gt, cosv, sinv):
+    rows = []
+    for h in range(2):
+        o = h * HD
+        a, b = gt[o : o + 8], gt[o + 8 : o + 16]
+        rows += [a * cosv + b * sinv, b * cosv - a * sinv, gt[o + 16 : o + HD]]
+    return jnp.concatenate(rows, 0)
 
 
 def attend_backward_kernel(
-    last_ref, q_ref, k_ref, v_ref, do_ref, raw_ref, lse_ref, rng_ref, c_ref, s1_ref, s2_ref,
+    last_ref, q_ref, k_ref, v_ref, do_ref, raw_ref, lse_ref, rng_ref, cs_ref,
     out_ref, kt_ref, dqt_ref, delta_ref,
 ):
     n = q_ref.shape[0]
@@ -155,7 +160,7 @@
         zero = jnp.zeros((BK, 128), F32)
         dk, dv = lax.fori_loop(k0 // BQ, last_ref[kb], q_step, (zero, zero))
         at = pl.ds(k0, BK)
-        out_ref[at, 128:256] = rope_back(dk, c_ref[at, :], s1_ref[at, :], s2_ref[at, :]).astype(BF)
+        out_ref[at, 128:256] = unrope(dk.T, cs_ref[0:8, at], cs_ref[8:16, at]).T.astype(BF)
         out_ref[at, 256:384] = dv.astype(BF)
         return 0
 
@@ -163,20 +168,20 @@
 
     def finish(i, _):
         at = pl.ds(pl.multiple_of(i * BQ, BQ), BQ)
-        dq = dqt_ref[:, at].T * (1.0 / math.sqrt(HD))
-        out_ref[at, 0:128] = rope_back(dq, c_ref[at, :], s1_ref[at, :], s2_ref[at, :]).astype(BF)
+        dq = dqt_ref[:, at] * (1.0 / math.sqrt(HD))
+        out_ref[at, 0:128] = unrope(dq, cs_ref[0:8, at], cs_ref[8:16, at]).T.astype(BF)
         return 0
 
     lax.fori_loop(0, n // BQ, finish, 0)
 
 
-def attend_backward(last, q, k, v, do, raw, lse, rng, c, s1, s2):
+def attend_backward(last, q, k, v, do, raw, lse, rng, cs):
     n = q.shape[0]
     return pl.pallas_call(
         attend_backward_kernel,
         name="attend_backward",
         out_shape=jax.ShapeDtypeStruct((n, 384), BF),
-        in_specs=[smem()] + [vmem()] * 10,
+        in_specs=[smem()] + [vmem()] * 8,
         out_specs=vmem(),
         scratch_shapes=[
             pltpu.VMEM((128, n), BF),
@@ -184,23 +189,390 @@
             pltpu.VMEM((8, n), F32),
         ],
         compiler_params=pltpu.CompilerParams(vmem_limit_bytes=56 * 2**20),
-    )(last, q, k, v, do, raw, lse, rng, c, s1, s2)
-
-
-def rope_tables(pos):
-    half = ROT // 2
-    freq = 10000.0 ** (-(jnp.arange(half, dtype=F32) * 2.0 / ROT))
-    ang = pos.astype(F32)[None, :] * freq[:, None]
-    cs, sn = lax.optimization_barrier((jnp.cos(ang), jnp.sin(ang)))
-    cs, sn = cs.T, sn.T
-    n = pos.shape[0]
-    one = jnp.ones((n, HD - ROT), F32)
-    zero = jnp.zeros((n, HD - ROT), F32)
-    z8 = jnp.zeros((n, half), F32)
-    c = jnp.concatenate([cs, cs, one] * 2, 1)
-    s1 = jnp.concatenate([-sn, z8, zero] * 2, 1)
-    s2 = jnp.concatenate([z8, sn, zero] * 2, 1)
-    return c, s1, s2
+    )(last, q, k, v, do, raw, lse, rng, cs)
+
+
+MESH = pl.DeviceIdType.MESH
+TC = 256
+XC = 2
+
+
+def hbm():
+    return pl.BlockSpec(memory_space=pl.ANY)
+
+
+def remote(src, dst, send, recv, dev):
+    return pltpu.make_async_remote_copy(
+        src_ref=src, dst_ref=dst, send_sem=send, recv_sem=recv, device_id=dev, device_id_type=MESH
+    )
+
+
+def where():
+    return lax.axis_index("dp"), lax.axis_index("row"), lax.axis_index("col")
+
+
+def greet(dp, row, col, rows=4, dps=4):
+    bar = pltpu.get_barrier_semaphore()
+    count = 0
+    for d in range(1, dps):
+        pl.semaphore_signal(bar, inc=1, device_id=(dp ^ d, row, col), device_id_type=MESH)
+        count += 1
+    for d in range(1, rows):
+        pl.semaphore_signal(bar, inc=1, device_id=(dp, lax.rem(row + d, rows), col), device_id_type=MESH)
+        count += 1
+    pl.semaphore_signal(bar, inc=1, device_id=(dp, row, 1 - col), device_id_type=MESH)
+    pl.semaphore_wait(bar, count + 1)
+
+
+class LineGather:
+    def __init__(self, own, full, sems, pos, half):
+        self.own, self.full, self.pos, self.half = own, full, pos, half
+        (self.su, self.sd, self.ru, self.rd, self.ss, self.rs, self.loc) = sems
+        self.piece = half // XC
+
+    def at(self, block, k):
+        dp, row, col = self.pos
+        start = pl.multiple_of(col * self.half + k * self.piece, self.piece)
+        return self.full.at[block, pl.ds(start, self.piece)]
+
+    def sib_at(self, block, k):
+        dp, row, col = self.pos
+        start = pl.multiple_of((1 - col) * self.half + k * self.piece, self.piece)
+        return self.full.at[block, pl.ds(start, self.piece)]
+
+    def src(self, step, block, k):
+        return self.own.at[pl.ds(k * self.piece, self.piece)] if step == 0 else self.at(block, k)
+
+    def up(self, step, k):
+        dp, row, col = self.pos
+        return remote(
+            self.src(step, row - step, k), self.at(row - step, k),
+            self.su.at[step, k], self.ru.at[step, k], (dp, row + 1, col),
+        )
+
+    def down(self, step, k):
+        dp, row, col = self.pos
+        return remote(
+            self.src(step, row + step, k), self.at(row + step, k),
+            self.sd.at[step, k], self.rd.at[step, k], (dp, row - 1, col),
+        )
+
+    def sib(self, step, sign, k):
+        dp, row, col = self.pos
+        i = step + 3 * (sign < 0)
+        block = row - sign * step
+        return remote(
+            self.src(step, block, k), self.at(block, k),
+            self.ss.at[i, k], self.rs.at[i, k], (dp, row, 1 - col),
+        )
+
+    def local(self):
+        dp, row, col = self.pos
+        start = pl.multiple_of(col * self.half, self.half)
+        return pltpu.make_async_copy(self.own, self.full.at[row, pl.ds(start, self.half)], self.loc)
+
+    def start(self):
+        dp, row, col = self.pos
+        for k in range(XC):
+            @pl.when(row < 3)
+            def _():
+                self.up(0, k).start()
+
+            @pl.when(row > 0)
+            def _():
+                self.down(0, k).start()
+        for k in range(XC):
+            self.sib(0, 1, k).start()
+        self.local().start()
+
+    def step(self, s):
+        dp, row, col = self.pos
+        for k in range(XC):
+            @pl.when(row >= s)
+            def _():
+                pltpu.make_async_copy(self.at(row - s, k), self.at(row - s, k), self.ru.at[s - 1, k]).wait()
+
+                @pl.when(row < 3)
+                def _():
+                    self.up(s, k).start()
+
+                self.sib(s, 1, k).start()
+
+            @pl.when(row + s <= 3)
+            def _():
+                pltpu.make_async_copy(self.at(row + s, k), self.at(row + s, k), self.rd.at[s - 1, k]).wait()
+
+                @pl.when(row > 0)
+                def _():
+                    self.down(s, k).start()
+
+                self.sib(s, -1, k).start()
+
+    def sib_wait(self, s, sign):
+        dp, row, col = self.pos
+        block = row - sign * s
+        i = s + 3 * (sign < 0)
+        for k in range(XC):
+            pltpu.make_async_copy(self.sib_at(block, k), self.sib_at(block, k), self.rs.at[i, k]).wait()
+
+    def arrived(self):
+        dp, row, col = self.pos
+        self.local().wait()
+        self.sib_wait(0, 1)
+        for s in range(1, 4):
+            @pl.when(row >= s)
+            def _():
+                self.sib_wait(s, 1)
+
+            @pl.when(row + s <= 3)
+            def _():
+                self.sib_wait(s, -1)
+
+    def drain(self):
+        dp, row, col = self.pos
+        for k in range(XC):
+            self.sib(0, 1, k).wait_send()
+            for s in range(0, 3):
+                @pl.when((row >= s) & (row < 3))
+                def _():
+                    self.up(s, k).wait_send()
+
+                @pl.when((row + s <= 3) & (row > 0))
+                def _():
+                    self.down(s, k).wait_send()
+            for s in range(1, 4):
+                @pl.when(row >= s)
+                def _():
+                    self.sib(s, 1, k).wait_send()
+
+                @pl.when(row + s <= 3)
+                def _():
+                    self.sib(s, -1, k).wait_send()
+
+
+def line_sems():
+    dma = pltpu.SemaphoreType.DMA
+    return [dma((4, XC))] * 4 + [dma((7, XC))] * 2 + [dma]
+
+
+class WeightGather:
+    def __init__(self, packed, full, sems, pos):
+        self.packed, self.full, self.pos = packed, full, pos
+        self.sz, self.rz, self.sp, self.rp, self.loc = sems
+        self.rows = packed.shape[1] // 4
+
+    def part(self, ref, block, quarter):
+        return ref.at[block, pl.ds(pl.multiple_of(quarter * self.rows, self.rows), self.rows)]
+
+    def along(self, d):
+        dp, row, col = self.pos
+        target = lax.rem(row + d, 4)
+        return remote(
+            self.part(self.packed, target, dp), self.part(self.full, row, dp),
+            self.sz.at[d], self.rz.at[d], (dp, target, col),
+        )
+
+    def across(self, d, e):
+        dp, row, col = self.pos
+        block = lax.rem(row + 4 - d, 4)
+        return remote(
+            self.part(self.full, block, dp), self.part(self.full, block, dp),
+            self.sp.at[d, e], self.rp.at[d, e], (dp ^ e, row, col),
+        )
+
+    def local(self):
+        dp, row, col = self.pos
+        return pltpu.make_async_copy(self.packed.at[row], self.full.at[row], self.loc)
+
+    def start(self):
+        for d in (2, 1, 3):
+            self.along(d).start()
+        self.local().start()
+
+    def forward(self):
+        dp, row, col = self.pos
+        for d in (1, 3, 2):
+            block = lax.rem(row + 4 - d, 4)
+            part = self.part(self.full, block, dp)
+            pltpu.make_async_copy(part, part, self.rz.at[d]).wait()
+            for e in (3, 1, 2):
+                self.across(d, e).start()
+
+    def arrived(self):
+        dp, row, col = self.pos
+        self.local().wait()
+        for d in (1, 3, 2):
+            block = lax.rem(row + 4 - d, 4)
+            for e in (1, 2, 3):
+                part = self.part(self.full, block, dp ^ e)
+                pltpu.make_async_copy(part, part, self.rp.at[d, e]).wait()
+
+    def drain(self):
+        for d in (1, 2, 3):
+            self.along(d).wait_send()
+            for e in (1, 2, 3):
+                self.across(d, e).wait_send()
+
+
+def weight_sems():
+    dma = pltpu.SemaphoreType.DMA
+    return [dma((4,))] * 2 + [dma((4, 4))] * 2 + [dma]
+
+
+def project_kernel(
+    x, w1s, w2s, gb, seg, b1,
+    q_o, k_o, v_o, act_o, gp_o, nrm_o, w1_o, w2_o, stat_o, cs_o, rng_o,
+    xf, w1, w2, gbs, q_v, k_v, v_v, act_v, gp_v, nrm_v, stat_v, cs_v, rng_v, c_v, s1_v, s2_v,
+    *sems,
+):
+    pos = where()
+    dp, row, col = pos
+    toks = seg.shape[1]
+    half = toks // 2
+    line = LineGather(x, xf, sems[:7], pos, half)
+    g1 = WeightGather(w1s, w1, sems[7:12], pos)
+    g2 = WeightGather(w2s, w2, sems[12:17], pos)
+    gs, gr, out_sem = sems[17:20]
+    greet(dp, row, col)
+    g1.start()
+    line.start()
+
+    def gain_copy(d):
+        return remote(gb, gbs.at[row], gs.at[d], gr.at[d], (dp, lax.rem(row + d, 4), col))
+
+    for d in (1, 2, 3):
+        gain_copy(d).start()
+    own_gain = pltpu.make_async_copy(gb, gbs.at[row], gr.at[0])
+    own_gain.start()
+    g2.start()
+
+    labels = seg[...]
+    start = jnp.zeros_like(labels)
+    for d in range(1, 8):
+        below = jnp.sum((labels == d - 1).astype(F32), 1, keepdims=True).astype(jnp.int32)
+        start = start + jnp.where(labels >= d, below, 0)
+    index = lax.broadcasted_iota(jnp.int32, labels.shape, 1)
+    place = index - start
+    rng_v[0:1, :] = start
+    rng_v[1:2, :] = place
+    rng_v[2:8, :] = jnp.zeros((6, toks), jnp.int32)
+    power = lax.broadcasted_iota(jnp.int32, (8, 1), 0).astype(F32) * (-2.0 * math.log(10000.0) / ROT)
+    ang = place.astype(F32) * jnp.exp(power)
+    cs_v[0:8, :] = jnp.cos(ang)
+    cs_v[8:16, :] = jnp.sin(ang)
+
+    def table_step(i, _):
+        at = pl.ds(pl.multiple_of(i * TC, TC), TC)
+        cosv, sinv = cs_v[0:8, at], cs_v[8:16, at]
+        one = jnp.ones((HD - ROT, TC), F32)
+        zero = jnp.zeros((HD - ROT, TC), F32)
+        z8 = jnp.zeros((8, TC), F32)
+        c_v[at, :] = jnp.concatenate([cosv, cosv, one] * 2, 0).T
+        s1_v[at, :] = jnp.concatenate([-sinv, z8, zero] * 2, 0).T
+        s2_v[at, :] = jnp.concatenate([z8, sinv, zero] * 2, 0).T
+        return 0
+
+    lax.fori_loop(0, toks // TC, table_step, 0)
+
+    line.step(1)
+    g1.forward()
+    line.step(2)
+    line.step(3)
+    g2.forward()
+    own_gain.wait()
+    for d in (1, 2, 3):
+        src = gbs.at[lax.rem(row + 4 - d, 4)]
+        pltpu.make_async_copy(src, src, gr.at[d]).wait()
+    line.arrived()
+    g1.arrived()
+
+    def out(i, src, dst):
+        return pltpu.make_async_copy(src, dst, out_sem.at[i])
+
+    out(7, w1, w1_o).start()
+    bias = b1[...]
+
+    def token_step(i, _):
+        at = pl.ds(pl.multiple_of(i * TC, TC), TC)
+        blocks = [xf[b, at, :].astype(F32) for b in range(4)]
+        total = (blocks[0] + blocks[1]) + (blocks[2] + blocks[3])
+        square = (blocks[0] * blocks[0] + blocks[1] * blocks[1]) + (
+            blocks[2] * blocks[2] + blocks[3] * blocks[3]
+        )
+        mean = jnp.sum(total, 1, keepdims=True) * (1.0 / D)
+        var = jnp.sum(square, 1, keepdims=True) * (1.0 / D) - mean * mean
+        inv = lax.rsqrt(var + EPSILON)
+        lane = lax.broadcasted_iota(jnp.int32, (TC, 128), 1)
+        stat_v[at, :] = jnp.where(lane == 0, mean, inv)
+        acc = None
+        for b in range(4):
+            gain = gbs[b, 0:1, :]
+            shift = gbs[b, 1:2, :]
+            n = ((blocks[b] - mean) * inv * gain + shift).astype(BF)
+            nrm_v[b, at, :] = n
+            part = dot(n, w1[b])
+            acc = part if acc is None else acc + part
+        acc = acc + bias
+        c, s1, s2 = c_v[at, :], s1_v[at, :], s2_v[at, :]
+        q_v[at, :] = rope(acc[:, 0:128], c, s1, s2).astype(BF)
+        k_v[at, :] = rope(acc[:, 128:256], c, s1, s2).astype(BF)
+        v_v[at, :] = acc[:, 256:384].astype(BF)
+        up = acc[:, 384:]
+        phi = 0.5 * (1.0 + lax.erf(up * (1.0 / math.sqrt(2.0))))
+        act_v[at, :] = (up * phi).astype(BF)
+        gp_v[at, :] = (phi + up * jnp.exp(-0.5 * up * up) * (1.0 / math.sqrt(2.0 * math.pi))).astype(BF)
+        return 0
+
+    lax.fori_loop(0, toks // TC, token_step, 0)
+    own = stat_v.at[pl.ds(pl.multiple_of(col * half, half), half)]
+    pairs = [
+        (q_v, q_o), (k_v, k_o), (v_v, v_o), (act_v, act_o), (gp_v, gp_o), (nrm_v, nrm_o),
+        (own, stat_o), (w1, w1_o), (cs_v, cs_o), (rng_v, rng_o),
+    ]
+    for i, (s, d) in enumerate(pairs):
+        if i != 7:
+            out(i, s, d).start()
+    g2.arrived()
+    out(10, w2, w2_o).start()
+    line.drain()
+    g1.drain()
+    g2.drain()
+    for d in (1, 2, 3):
+        gain_copy(d).wait_send()
+    for i, (s, d) in enumerate(pairs):
+        out(i, s, d).wait()
+    out(10, w2, w2_o).wait()
+
+
+def project(x, w1s, w2s, gb, seg, b1):
+    toks = seg.shape[1]
+    nw1, nw2 = w1s.shape, w2s.shape
+    fc = nw1[2] - 384
+    dma = pltpu.SemaphoreType.DMA
+    sd = jax.ShapeDtypeStruct
+    return pl.pallas_call(
+        project_kernel,
+        name="project",
+        out_shape=(
+            sd((toks, 128), BF), sd((toks, 128), BF), sd((toks, 128), BF), sd((toks, fc), BF),
+            sd((toks, fc), BF), sd((4, toks, 256), BF), sd(nw1, BF), sd(nw2, BF),
+            sd((toks // 2, 128), F32), sd((16, toks), F32), sd((8, toks), jnp.int32),
+        ),
+        in_specs=[hbm()] * 3 + [vmem()] * 3,
+        out_specs=(hbm(),) * 11,
+        scratch_shapes=[
+            pltpu.VMEM((4, toks, 256), BF), pltpu.VMEM(nw1, BF), pltpu.VMEM(nw2, BF),
+            pltpu.VMEM((4, 8, 256), F32),
+            pltpu.VMEM((toks, 128), BF), pltpu.VMEM((toks, 128), BF), pltpu.VMEM((toks, 128), BF),
+            pltpu.VMEM((toks, fc), BF), pltpu.VMEM((toks, fc), BF), pltpu.VMEM((4, toks, 256), BF),
+            pltpu.VMEM((toks, 128), F32), pltpu.VMEM((16, toks), F32), pltpu.VMEM((8, toks), jnp.int32),
+            pltpu.VMEM((toks, 128), F32), pltpu.VMEM((toks, 128), F32), pltpu.VMEM((toks, 128), F32),
+            *line_sems(), *weight_sems(), *weight_sems(), dma((4,)), dma((4,)), dma((11,)),
+        ],
+        compiler_params=pltpu.CompilerParams(
+            collective_id=0, has_side_effects=True, vmem_limit_bytes=56 * 2**20
+        ),
+    )(x, w1s, w2s, gb, seg, b1)
 
 
 def per_device_sliced(
@@ -215,20 +587,12 @@
     half = inputs.shape[0]
 
     seg = segments[0]
-    idx = jnp.arange(toks, dtype=jnp.int32)
-    start = jnp.sum(
-        jnp.where(seg[None, :] < seg[:, None], 1, 0), 1, dtype=jnp.int32
-    )
-    pos = idx - start
-    c, s1, s2 = rope_tables(pos)
-    rng = jnp.concatenate([start[None], pos[None], jnp.zeros((6, toks), jnp.int32)], 0)
-    first = start[::BQ] // BK
-    ends = jnp.sum(jnp.where(start[None, :] <= idx[BK - 1 :: BK, None], 1, 0), 1, dtype=jnp.int32)
+    first = jnp.sum((seg[None, :] < seg[::BQ, None]).astype(jnp.int32), 1) // BK
+    ends = jnp.sum((seg[None, :] <= seg[BK - 1 :: BK, None]).astype(jnp.int32), 1)
     last = (ends + BQ - 1) // BQ
 
-    xg = lax.all_gather(lax.all_gather(inputs, "row"), "col", axis=1, tiled=True)
     cg = lax.all_gather(lax.all_gather(cotangent, "row"), "col", axis=1, tiled=True)
-    gb = lax.all_gather(jnp.stack([ln_gain, ln_bias]).astype(F32), "row")
+    gb = jnp.concatenate([ln_gain[None], ln_bias[None], jnp.zeros((6, dpart), BF)]).astype(F32)
     w1s = jnp.concatenate(
         [
             w_qkv.reshape(dpart, 3, nrow, hcols).transpose(2, 0, 1, 3).reshape(nrow, dpart, 3 * hcols),
@@ -239,8 +603,6 @@
     w2s = jnp.concatenate(
         [w_out.reshape(nrow, hcols, dpart), w_down.reshape(nrow, fcols, dpart)], 1
     )
-    w1 = lax.all_to_all(w1s, "row", 0, 0)
-    w2 = lax.all_to_all(w2s, "row", 0, 0)
     b1 = jnp.concatenate(
         [
             lax.dynamic_slice_in_dim(b_qkv, row * hcols, hcols, 1).reshape(-1),
@@ -248,26 +610,10 @@
         ]
     ).astype(F32)
 
-    xf = xg.astype(F32)
-    mean = jnp.sum(xf, (0, 2)) / D
-    var = jnp.sum(xf * xf, (0, 2)) / D - mean * mean
-    inv = lax.rsqrt(var + EPSILON)
-    xhat = (xf - mean[None, :, None]) * inv[None, :, None]
-    normed = (xhat * gb[:, 0:1] + gb[:, 1:2]).astype(BF)
-    nd = normed.transpose(1, 0, 2).reshape(toks, D)
-    proj = dot(nd, w1.reshape(D, -1)) + b1
     h3 = 3 * hcols
-
-    def rp(x):
-        return (
-            x * c + jnp.roll(x, -8, 1) * s1 + jnp.roll(x, 8, 1) * s2
-        ).astype(BF)
-
-    q, k, v = rp(proj[:, :hcols]), rp(proj[:, hcols : 2 * hcols]), proj[:, 2 * hcols : h3].astype(BF)
-    up = proj[:, h3:]
-    phi = 0.5 * (1.0 + lax.erf(up * (1.0 / math.sqrt(2.0))))
-    act = (up * phi).astype(BF)
-    gp = phi + up * jnp.exp(-0.5 * up * up) * (1.0 / math.sqrt(2.0 * math.pi))
+    q, k, v, act, gp, nrm, w1, w2, stat, cs, rng = project(
+        inputs, w1s, w2s, gb, segments, b1[None]
+    )
     attended, raw, lse = attend_forward(first, q, k, v, rng)
 
     joined = jnp.concatenate([attended, act], 1)
@@ -283,14 +629,15 @@
     dj = dot(cgd, w2d, NT)
     datt = dj[:, :hcols].astype(BF)
     dup = (dj[:, hcols:] * gp).astype(BF)
-    dproj = attend_backward(last, q, k, v, datt, raw, lse, rng, c, s1, s2)
+    dproj = attend_backward(last, q, k, v, datt, raw, lse, rng, cs)
     d1 = jnp.concatenate([dproj, dup], 1)
+    nd = nrm.transpose(1, 0, 2).reshape(toks, D)
     g1 = dot(nd, d1, TN)
     gb1 = jnp.sum(d1.astype(F32), 0)
     dn = jnp.einsum("tn,bkn->btk", d1, w1, preferred_element_type=F32).astype(BF)
     dn = lax.psum_scatter(dn, "row", scatter_dimension=0)
     dn = lax.psum_scatter(dn, "col", scatter_dimension=0, tiled=True).astype(F32)
-    myx = lax.dynamic_slice_in_dim(mean, col * half, half), lax.dynamic_slice_in_dim(inv, col * half, half)
+    myx = stat[:, 0], stat[:, 1]
     xh = (inputs.astype(F32) - myx[0][:, None]) * myx[1][:, None]
     dc = dn * ln_gain.astype(F32)
     st = lax.psum((jnp.sum(dc, 1), jnp.sum(dc * xh, 1)), "row")

time: 678 us -> 604 us (0.89)
  blocking collectives: 108 us -> 50.2 us
  Pallas kernels: 55.5 us -> 106 us
  other arithmetic: 31.9 us -> 12.7 us
  local copies, waits for them, and re-layouts: 61.9 us -> 46.5 us
  waiting for transfers between devices: 341 us -> 326 us
  starting transfers between devices: 22.4 us -> 13.2 us
    pallas_call x0 -> x1, Pallas kernels: none -> 66.2 us  [project(): pl.pallas_call(project_kernel, name='project', out_shape=(sd((toks, 128),...]
    all_gather x1 -> x0, blocking collectives: 58.3 us -> none  [per_device_sliced(): gb = lax.all_gather(jnp.stack([ln_gain, ln_bias]).astype(F32), 'row')]
    all_gather x2 -> x0, waiting for transfers between devices: 54.1 us -> none  [the longest x1 49.5 us: per_device_sliced(): lax.all_gather(inputs, 'row')]
    all_gather x1, waiting for transfers between devices: 0.02 us -> 50.3 us  [per_device_sliced(): lax.all_gather(cotangent, 'row')]
    all_to_all x2 -> x0, waiting for transfers between devices: 17.4 us -> none  [the longest x1 17.4 us: per_device_sliced(): w2 = lax.all_to_all(w2s, 'row', 0, 0)]
    pallas_call x1, Pallas kernels: 36 us -> 22.6 us  [attend_backward(): pl.pallas_call(attend_backward_kernel, name='attend_backward', out_shape=...]
    concatenate x4 -> x2, local copies, waits for them, and re-layouts: 11.9 us -> 1.56 us  [the longest x1 1.49 us: per_device_sliced(): joined = jnp.concatenate([attended, act], 1)]
    all_to_all x2 -> x0, starting transfers between devices: 9.21 us -> none  [the longest x1 4.8 us: per_device_sliced(): w2 = lax.all_to_all(w2s, 'row', 0, 0)]
  transfers between devices with their start and end apart: 13 -> 9, of which waited for: 6 -> 4; matrix products, arithmetic and copies ran while one was open for 12% -> 9% of each run, Pallas kernels for 0% -> 14%
where the time goes in v2:
time: 604 us; the launch traced here: 603 us
  waiting for transfers between devices  326 us (54%)
  Pallas kernels  106 us (18%)
  blocking collectives  50.2 us (8%)
  local copies, waits for them, and re-layouts  46.5 us (8%)
  matrix products  34.1 us (6%)
  between operations  14.5 us (2%)
  starting transfers between devices  13.2 us (2%)
  other arithmetic  12.7 us (2%)
    reduce_scatter x1, waiting for transfers between devices, per_device_sliced(): outp = lax.psum_scatter(outp, 'row', scatter_dimension=0)  105 us
    reduce_scatter x1, waiting for transfers between devices, per_device_sliced(): dn = lax.psum_scatter(dn, 'row', scatter_dimension=0)  93.6 us
    psum x1, waiting for transfers between devices, per_device_sliced(): g1 = lax.psum(g1.astype(BF), 'dp').reshape(nrow, dpart, -1)  76.2 us
    pallas_call x1, Pallas kernels, project(): pl.pallas_call(project_kernel, name='project', out_shape=(sd((toks, 128),...  66.2 us
    all_gather x1, waiting for transfers between devices, per_device_sliced(): lax.all_gather(cotangent, 'row')  50.3 us
    pallas_call x1, Pallas kernels, attend_backward(): pl.pallas_call(attend_backward_kernel, name='attend_backward', out_shape=...  22.6 us
    all_gather x1, blocking collectives, per_device_sliced(): gb1 = lax.all_gather(lax.psum(gb1, 'dp'), 'row')  18.9 us
    dot_general x3, matrix products, dot(): return lax.dot_general(a, b, dims, preferred_element_type=F32)  18.4 us
  transfers between devices with their start and end apart: 9, of which 4 were waited for; matrix products, arithmetic and copies ran while one was open for 9% of the time, Pallas kernels for 14%

profile of v2, /device:TPU:0, one launch (start us, length us, event | category | flops | bytes accessed | tf_op | source)
XLA Modules:
  0.0 602.8 jit_solution(7096252780580943576)
XLA Ops:
  8.0 50.3 %all-gather.7.cloned.1.call-done = bf16[4096,256]{1,0:T(8,128)(2,1)} async-done(((bf16[1024,256]{1,0:T(8,128)(2,1)}), bf16[4096,256]{1,0:T(8,128)(2,1)}) %all-gather.7.cloned.1.call-update) | async-done | bytes 2097168 | tf_op jit(solution)/shard_map/all_gather | solution.py:594
  63.3 2.5 pad_maximum_fusion.2.w2s
  67.9 66.2 %project.1 = (bf16[2048,128]{1,0:T(8,128)(2,1)}, bf16[2048,128]{1,0:T(8,128)(2,1)}, bf16[2048,128]{1,0:T(8,128)(2,1)}, bf16[2048,512]{1,0:T(8,128)(2,1)}, bf16[2...) custom-call(bf16[1024,256]{1,0:T(8,128)(2,1)} %x.1, ...), custom_call_target="tpu_custom_call" | custom-call | tf_op jit(solution)/shard_map/project/pallas_call | solution.py:553
  134.1 6.4 %copy.114 = bf16[2048,4,256]{0,2,1:T(8,128)(2,1)} copy(bf16[2048,4,256]{2,0,1:T(8,128)(2,1)} %bitcast.85) | data formatting | bytes 8388608 | tf_op jit(solution)/shard_map/transpose | solution.py:634
  140.8 16.8 %attend_forward.1 = (bf16[2048,128]{1,0:T(8,128)(2,1)S(1)}, f32[128,2048]{1,0:T(8,128)S(1)}, f32[8,2048]{1,0:T(8,128)S(1)}) custom-call(s32[4]{0:T(128)S(1)} %and_select_fusion.1.first_ref, bf16[2048,128]{1,0:T(8,128)(2,1)S(1)} %copy-done.2, bf16[2048,128]{1,0:T(8,128)(2,1)S(1)} %copy-done.3, bf16[2048,128]{1,0:T(8,128)(2,1)S(1)} %copy-done.4, ...), custom_call_target="tpu_custom_call" | custom-call | tf_op jit(solution)/shard_map/attend_forward/pallas_call | solution.py:90
  161.7 5.4 convolution_bitcast_fusion
  168.5 22.6 %attend_backward.1 = bf16[2048,384]{1,0:T(8,128)(2,1)} custom-call(s32[8]{0:T(128)} %and_select_fusion.last_ref, bf16[2048,128]{1,0:T(8,128)(2,1)} %get-tuple-element.26.q_ref, bf16[2048,128]{1,0:T(8,128)(2,1)} %get-tuple-element.27.k_ref, bf16[2048,128]{1,0:T(8,128)(2,1)} %get-tuple-element.28.v_ref, bf16[2048,128]{1,0:T(8,128)(2,1)} %slice.65.do_ref, ...), custom_call_target="tpu_custom_call" | custom-call | tf_op jit(solution)/shard_map/attend_backward/pallas_call | solution.py:180
  191.1 7.1 %convolution_convert_fusion = bf16[1024,896]{1,0:T(8,128)(2,1)} fusion(bf16[2048,1024]{0,1:T(8,128)(2,1)S(1)} %bitcast.84, bf16[2048,512]{1,0:T(8,128)(2,1)S(1)} %fusion, bf16[2048,384]{1,0:T(8,128)(2,1)} %attend_backward.1), kind=kOutput, calls=%fused_computation.10 | convolution fusion | flops 3766353920 | bytes 9699328 | tf_op jit(solution)/shard_map/dot_general | solution.py:24
  198.2 3.6 copy.115
  201.8 6.2 %copy.117 = bf16[2048,4,256]{0,2,1:T(8,128)(2,1)} copy(bf16[2048,4,256]{2,0,1:T(8,128)(2,1)} %bitcast.83) | data formatting | bytes 8388608 | tf_op jit(solution)/shard_map/transpose | solution.py:626
  208.0 5.9 convolution_convert_fusion.1
  215.2 8.4 %convert_bitcast_fusion = bf16[4,2048,256]{1,2,0:T(8,128)(2,1)} fusion(bf16[4,256,896]{2,1,0:T(8,128)(2,1)} %get-tuple-element.33, bf16[2048,512]{1,0:T(8,128)(2,1)S(1)} %fusion, bf16[2048,384]{1,0:T(8,128)(2,1)} %attend_backward.1), kind=kOutput, calls=%fused_computation.3 | convolution fusion | flops 3767533568 | bytes 9699328 | tf_op jit(solution)/shard_map/tn,bkn->btk/dot_general | solution.py:637
  223.7 7.2 %convert_bitcast_fusion.1 = bf16[4,2048,256]{1,2,0:T(8,128)(2,1)} fusion(bf16[4,640,256]{2,1,0:T(8,128)(2,1)S(1)} %copy-done.18, bf16[2048,640]{1,0:T(8,128)(2,1)} %constant_dynamic-update-slice_fusion), kind=kOutput, calls=%fused_computation.4 | convolution fusion | flops 2686451712 | bytes 8126464 | tf_op jit(solution)/shard_map/tk,bkn->btn/dot_general | solution.py:621
  230.9 76.2 %all-reduce.5.cloned.1.call-done = (bf16[4,256,896]{1,2,0:T(8,128)(2,1)}, bf16[4,640,256]{2,1,0:T(8,128)(2,1)}) async-done(((bf16[4,256,896]{1,2,0:T(8,128)(2,1)}, bf16[4,640,256]{2,1,0:T(8,128)(2,1)}), (bf16[4,256,896]{1,2,0:T(8,128)(2,1)}, bf16[4,640,256]{2,1,0:T(8,128)(2,1)})) %all-reduce.5.cloned.1.call-update) | async-done | bytes 3145744 | tf_op jit(solution)/shard_map/psum | solution.py:649
  307.1 4.6 all-to-all-start.1
  311.7 93.6 %reduce-scatter.9.cloned.1.call-done = bf16[1,2048,256]{1,2,0:T(8,128)(2,1)} async-done(((bf16[4,2048,256]{1,2,0:T(8,128)(2,1)}), bf16[1,2048,256]{1,2,0:T(8,128)(2,1)}) %reduce-scatter.9.cloned.1.call-update) | async-done | bytes 1048592 | tf_op jit(solution)/shard_map/reduce_scatter | solution.py:638
  405.4 8.4 %all-to-all-start = ((bf16[4,256,896]{1,2,0:T(8,128)(2,1)}), bf16[4,256,896]{1,2,0:T(8,128)(2,1)S(1)}, u32[]{:S(2)}, u32[]{:S(2)}) async-start(bf16[4,256,896]{1,2,0:T(8,128)(2,1)} %get-tuple-element.116), calls=%async_computation.4 | async-start | bytes 3670016 | tf_op jit(solution)/shard_map/all_to_all | solution.py:651
  413.7 105.1 %reduce-scatter.5.cloned.1.call-done = bf16[1,2048,256]{1,2,0:T(8,128)(2,1)} async-done(((bf16[4,2048,256]{1,2,0:T(8,128)(2,1)}), bf16[1,2048,256]{1,2,0:T(8,128)(2,1)}) %reduce-scatter.5.cloned.1.call-update) | async-done | bytes 1048592 | tf_op jit(solution)/shard_map/reduce_scatter | solution.py:622
  518.9 2.0 copy.113
  520.9 2.0 copy.105
  523.0 1.7 slice_reduce_fusion.1
  524.7 2.6 convert_reduce_fusion
  527.3 8.9 %psum.61 = f32[1,896]{1,0:T(1,128)S(1)} all-reduce(f32[1,896]{1,0:T(1,128)S(1)} %all_gather.18), channel_id=1, replica_groups=mesh['dp'=4,'row'=4,'col'=2] {'dp'}, use_global_device_ids=true, to_apply=%region_16.17 | all-reduce | flops 896 | bytes 7168 | tf_op jit(solution)/shard_map/psum | solution.py:653
  536.2 18.9 %all-gather.1 = f32[4,1,896]{2,1,0:T(1,128)S(1)} all-gather(f32[1,1,896]{2,1,0:T(1,128)S(1)} %bitcast.105), channel_id=1, replica_groups=mesh['dp'=4,'row'=4,'col'=2] {'row'}, dimensions={0}, use_global_device_ids=true | all-gather | bytes 17920 | tf_op jit(solution)/shard_map/all_gather | solution.py:653
  557.2 1.5 slice.56
  560.1 3.0 copy.121
  563.2 1.5 slice.54
  564.7 3.0 copy.122
  567.7 1.5 fusion.15
  569.2 10.0 %all-reduce.1 = (f32[1024]{0:T(1024)S(1)}, f32[1024]{0:T(1024)S(1)}) all-reduce(f32[1024]{0:T(1024)S(1)} %get-tuple-element.106, f32[1024]{0:T(1024)S(1)} %get-tuple-element.107), channel_id=1, replica_groups=mesh['dp'=4,'row'=4,'col'=2] {'row'}, use_global_device_ids=true, to_apply=%region_9.10 | all-reduce | flops 2048 | bytes 16384 | tf_op jit(solution)/shard_map/psum | solution.py:643
  579.3 2.0 convert_reduce_fusion.2
  583.6 12.3 %all-reduce = (f32[256]{0:T(256)}, f32[256]{0:T(256)}, f32[256]{0:T(256)}) all-reduce(f32[256]{0:T(256)S(1)} %get-tuple-element.105, f32[256]{0:T(256)S(1)} %get-tuple-element.108, f32[256]{0:T(256)S(1)} %get-tuple-element.118), channel_id=1, replica_groups=mesh['dp'=4,'row'=4,'col'=2] {'dp','col'}, use_global_device_ids=true, to_apply=%region_11.12 | all-reduce | flops 768 | bytes 6144 | tf_op jit(solution)/shard_map/psum | solution.py:647
  (104 shorter events, 20.6 us)
Async XLA Ops:
  7.2 55.5 %copy-start = (bf16[3,512]{1,0:T(4,128)(2,1)S(1)}, bf16[3,512]{1,0:T(4,128)(2,1)}, u32[]{:S(2)}) copy-start(bf16[3,512]{1,0:T(4,128)(2,1)} %param.17) | copy-start | bytes 9220
  7.2 52.8 %copy-start.14 = (bf16[256,2048]{1,0:T(8,128)(2,1)S(1)}, bf16[256,2048]{1,0:T(8,128)(2,1)}, u32[]{:S(2)}) copy-start(bf16[256,2048]{1,0:T(8,128)(2,1)} %param.19) | copy-start | bytes 3145732
  7.2 51.1 %all-gather.7.cloned.1.call-start = ((), (), s32[]{:S(2)}) async-start(), calls=%async_computation.11 | async-start | bytes 2621440 | tf_op jit(solution)/shard_map/all_gather | solution.py:594
  7.9 153.8 %all-gather.5.cloned.1.call-start = ((), (), s32[]{:S(2)}) async-start(), calls=%async_computation.8 | async-start | bytes 6291456 | tf_op jit(solution)/shard_map/all_gather | solution.py:594
  58.3 2.8 copy-start.15
  58.3 248.8 %all-reduce.5.cloned.1.call-start = ((), (), s32[]{:S(2)}) async-start(), calls=%async_computation.12 | async-start | bytes 6291456 | tf_op jit(solution)/shard_map/psum | solution.py:649
  61.1 0.7 copy-start.19
  61.1 0.7 copy-start.20
  61.1 2.2 copy-start.16
  134.1 6.4 %copy-start.17 = (s32[1,2048]{1,0:T(1,128)S(1)}, s32[1,2048]{1,0:T(1,128)}, u32[]{:S(2)}) copy-start(s32[1,2048]{1,0:T(1,128)} %seg.1) | copy-start | bytes 24580
  134.1 6.6 %copy-start.2 = (bf16[2048,128]{1,0:T(8,128)(2,1)S(1)}, bf16[2048,128]{1,0:T(8,128)(2,1)}, u32[]{:S(2)}) copy-start(bf16[2048,128]{1,0:T(8,128)(2,1)} %get-tuple-element.26.q_ref) | copy-start | bytes 1572868
  134.1 6.6 %copy-start.3 = (bf16[2048,128]{1,0:T(8,128)(2,1)S(1)}, bf16[2048,128]{1,0:T(8,128)(2,1)}, u32[]{:S(2)}) copy-start(bf16[2048,128]{1,0:T(8,128)(2,1)} %get-tuple-element.27.k_ref) | copy-start | bytes 1572868
  134.1 6.6 %copy-start.4 = (bf16[2048,128]{1,0:T(8,128)(2,1)S(1)}, bf16[2048,128]{1,0:T(8,128)(2,1)}, u32[]{:S(2)}) copy-start(bf16[2048,128]{1,0:T(8,128)(2,1)} %get-tuple-element.28.v_ref) | copy-start | bytes 1572868
  134.1 6.6 %copy-start.6 = (s32[8,2048]{1,0:T(8,128)S(1)}, s32[8,2048]{1,0:T(8,128)}, u32[]{:S(2)}) copy-start(s32[8,2048]{1,0:T(8,128)} %get-tuple-element.29.rng_ref) | copy-start | bytes 196612
  140.5 19.7 %copy-start.11 = (bf16[2048,512]{1,0:T(8,128)(2,1)S(1)}, bf16[2048,512]{1,0:T(8,128)(2,1)}, u32[]{:S(2)}) copy-start(bf16[2048,512]{1,0:T(8,128)(2,1)} %get-tuple-element.31) | copy-start | bytes 6291460
  157.6 1.0 copy-start.5
  158.6 1.6 copy-start.7
  159.3 2.4 copy-start.18
  161.7 6.3 %copy-start.12 = (bf16[2048,512]{1,0:T(8,128)(2,1)S(1)}, bf16[2048,512]{1,0:T(8,128)(2,1)}, u32[]{:S(2)}) copy-start(bf16[2048,512]{1,0:T(8,128)(2,1)} %get-tuple-element.37) | copy-start | bytes 6291460
  168.5 46.7 %copy-start.8 = (bf16[2048,512]{1,0:T(8,128)(2,1)}, bf16[2048,512]{1,0:T(8,128)(2,1)S(1)}, u32[]{:S(2)}) copy-start(bf16[2048,512]{1,0:T(8,128)(2,1)S(1)} %fusion) | copy-start | bytes 6291460
  168.5 22.6 %copy-start.10 = (bf16[2048,4,256]{0,2,1:T(8,128)(2,1)S(1)}, bf16[2048,4,256]{0,2,1:T(8,128)(2,1)}, u32[]{:S(2)}) copy-start(bf16[2048,4,256]{0,2,1:T(8,128)(2,1)} %copy.114) | copy-start | bytes 12582916
  215.1 190.2 %reduce-scatter.9.cloned.1.call-start = ((), (), s32[]{:S(2)}) async-start(), calls=%async_computation.9 | async-start | bytes 5242880 | tf_op jit(solution)/shard_map/reduce_scatter | solution.py:638
  223.6 295.2 %reduce-scatter.5.cloned.1.call-start = ((), (), s32[]{:S(2)}) async-start(), calls=%async_computation.6 | async-start | bytes 5242880 | tf_op jit(solution)/shard_map/reduce_scatter | solution.py:622
  307.1 98.2 %all-to-all-start.1 = ((bf16[4,640,256]{2,1,0:T(8,128)(2,1)}), bf16[4,640,256]{2,1,0:T(8,128)(2,1)S(1)}, u32[]{:S(2)}, u32[]{:S(2)}) async-start(bf16[4,640,256]{2,1,0:T(8,128)(2,1)} %get-tuple-element.117), calls=%async_computation.5 | async-start | bytes 2621440 | tf_op jit(solution)/shard_map/all_to_all | solution.py:652
  311.7 256.0 %reduce-scatter.11.cloned.1.call-start = ((), (), s32[]{:S(2)}) async-start(), calls=%async_computation.10 | async-start | bytes 1572864 | tf_op jit(solution)/shard_map/reduce_scatter | solution.py:639
  405.3 117.6 %copy-start.21 = (bf16[256]{0:T(256)(128)(2,1)S(1)}, bf16[256]{0:T(256)(128)(2,1)}, u32[]{:S(2)}) copy-start(bf16[256]{0:T(256)(128)(2,1)} %param.22) | copy-start | bytes 1540
  405.4 153.3 %all-to-all-start = ((bf16[4,256,896]{1,2,0:T(8,128)(2,1)}), bf16[4,256,896]{1,2,0:T(8,128)(2,1)S(1)}, u32[]{:S(2)}, u32[]{:S(2)}) async-start(bf16[4,256,896]{1,2,0:T(8,128)(2,1)} %get-tuple-element.116), calls=%async_computation.4 | async-start | bytes 3670016 | tf_op jit(solution)/shard_map/all_to_all | solution.py:651
  413.7 165.5 %reduce-scatter.7.cloned.1.call-start = ((), (), s32[]{:S(2)}) async-start(), calls=%async_computation.7 | async-start | bytes 1572864 | tf_op jit(solution)/shard_map/reduce_scatter | solution.py:623
  564.7 3.0 copy-start.9
  564.7 14.6 %copy-start.13 = (bf16[1024,256]{0,1:T(8,128)(2,1)S(1)}, bf16[1024,256]{0,1:T(8,128)(2,1)}, u32[]{:S(2)}) copy-start(bf16[1024,256]{0,1:T(8,128)(2,1)} %copy.113) | copy-start | bytes 1572868
  579.3 16.7 %copy-start.1 = (bf16[3,512]{1,0:T(4,128)(2,1)S(1)}, bf16[3,512]{1,0:T(4,128)(2,1)}, u32[]{:S(2)}) copy-start(bf16[3,512]{1,0:T(4,128)(2,1)} %param.17) | copy-start | bytes 9220
Sparse Core Ops, SparseCore 0:
  9.6 48.6 all-gather.6
  59.8 13.1 all-gather.4
  215.2 91.8 all-reduce.4
  309.3 95.9 reduce-scatter.8
  407.5 111.3 reduce-scatter.4
  521.0 13.1 reduce-scatter.10
  536.4 9.6 reduce-scatter.6
